TPU v7x, 32 devices: a whole 2x2x4 slice. The times are simulated.
32 devices in a mesh: grp: 4 (over x, core), ang: 8 (over z, y).
Axes of the slice: x: 2, y: 2, z: 4, core: 2. Of those that a mesh axis runs over, the one named last changes fastest.
Arguments:
- current: bfloat16 [2, 4096, 256], P(None, ('grp', 'ang')), may hold values from -6 to 6
- near_blocks: bfloat16 [1280, 2, 256, 256], P(('grp', 'ang')), may hold values from -0.25 to 0.25
- near_rows: int32 [1280], P(('grp', 'ang')), may hold values from 0 to 127
- near_cols: int32 [1280], P(('grp', 'ang')), may hold values from 0 to 1023
- radiate: float32 [2, 1024, 256], replicated, may hold values from -0.25 to 0.25
- receive: float32 [2, 1024, 256], replicated, may hold values from -0.109375 to 0.109375
- interp: float32 [1536, 1024], replicated, may hold values from -0.1875 to 0.1875
- shift_phase: float32 [8, 1536], replicated, may hold values from -3.140625 to 3.140625
- translate: float32 [2, 316, 1536], P(None, None, 'ang'), may hold values from -0.375 to 0.375
- far_sources: int32 [512, 16], P('grp'), may hold values from 0 to 511
- far_types: int32 [512, 16], P('grp'), may hold values from 0 to 315
Outputs:
- product: float32 [2, 4096, 256], P(None, ('grp', 'ang'))
Inputs may be any that keep to these rules, and one draw needn't show every extreme that they name: Block b is stored on device b div 40; near_rows[b] is one of that device's own 128 clusters. near_cols[b] is one of the 1024 clusters of block b's grp index, counted from that group's first cluster. `far_sources`: parent p holds leaf clusters 8 p to 8 p + 7; entries are global parent numbers. `far_types`: an index into the second dimension of translate.
All inputs are finite; a program needn't handle non-finite values.
Results may differ from a plain program's by a relative error of at most 0.0003.
Values may be sent and summed in bfloat16 or wider, within the bound.
No kernel may reach another device: no remote copies, remote signals or barrier semaphores. Data moves between devices by JAX's collectives and lax.ppermute only.
A program may use at most 128 MiB of HBM per device.

v0:
```python
import jax
import jax.numpy as jnp
from jax import lax
from jax.sharding import PartitionSpec as P

HIGHEST = lax.Precision.HIGHEST


def complex_product(formula, left_side, right_side):
    real_part = jnp.einsum(formula, left_side[0], right_side[0], precision=HIGHEST) - jnp.einsum(
        formula, left_side[1], right_side[1], precision=HIGHEST
    )
    imag_part = jnp.einsum(formula, left_side[0], right_side[1], precision=HIGHEST) + jnp.einsum(
        formula, left_side[1], right_side[0], precision=HIGHEST
    )
    return jnp.stack([real_part, imag_part])


def shift_sum(children, cosine, sine_part):
    grouped = children.reshape(2, children.shape[1], children.shape[2] // 8, 8)
    cos_t = cosine.T[:, None, :]
    sin_t = sine_part.T[:, None, :]
    real_part = jnp.sum(cos_t * grouped[0] - sin_t * grouped[1], axis=2)
    imag_part = jnp.sum(cos_t * grouped[1] + sin_t * grouped[0], axis=2)
    return jnp.stack([real_part, imag_part])


def spread(parents, cosine, sine_part):
    cos_t = cosine.T[:, None, :]
    sin_t = sine_part.T[:, None, :]
    par_real = parents[0][:, :, None]
    par_imag = parents[1][:, :, None]
    real_part = cos_t * par_real + sin_t * par_imag
    imag_part = cos_t * par_imag - sin_t * par_real
    width = parents.shape[2] * 8
    return jnp.stack(
        [real_part.reshape(parents.shape[1], width), imag_part.reshape(parents.shape[1], width)]
    )


def on_device(
    current,
    near_blocks,
    near_rows,
    near_cols,
    radiate,
    receive,
    interp,
    shift_phase,
    translate,
    far_sources,
    far_types,
):
    own_count = current.shape[1]
    gathered = lax.all_gather(current, "ang", axis=1, tiled=True)
    picked = jnp.take(gathered, near_cols, axis=1)
    blocks_real = near_blocks[:, 0]
    blocks_imag = near_blocks[:, 1]
    near_real = jnp.einsum(
        "bmn,bn->bm", blocks_real, picked[0], preferred_element_type=jnp.float32
    ) - jnp.einsum("bmn,bn->bm", blocks_imag, picked[1], preferred_element_type=jnp.float32)
    near_imag = jnp.einsum(
        "bmn,bn->bm", blocks_real, picked[1], preferred_element_type=jnp.float32
    ) + jnp.einsum("bmn,bn->bm", blocks_imag, picked[0], preferred_element_type=jnp.float32)
    onehot_rows = (near_rows[None, :] == jnp.arange(own_count, dtype=jnp.int32)[:, None]).astype(
        jnp.float32
    )
    near_part = jnp.einsum(
        "cb,sbm->scm", onehot_rows, jnp.stack([near_real, near_imag]), precision=HIGHEST
    )
    cosine = jnp.cos(shift_phase)
    sine_part = jnp.sin(shift_phase)
    own_values = current.astype(jnp.float32)
    radiated = complex_product("kn,cn->kc", radiate, own_values)
    children = jnp.einsum("jk,skc->sjc", interp, radiated, precision=HIGHEST)
    own_parents = shift_sum(children, cosine, sine_part)
    parents = lax.all_to_all(own_parents, "ang", split_axis=1, concat_axis=2, tiled=True)
    sources = lax.all_gather(parents, "grp", axis=2, tiled=True)
    kind_ids = jnp.arange(translate.shape[1], dtype=jnp.int32)
    parent_ids = jnp.arange(sources.shape[2], dtype=jnp.int32)
    list_len = far_sources.shape[1]

    def add_entry(slot_index, total):
        source_ids = lax.dynamic_index_in_dim(far_sources, slot_index, 1, False)
        type_ids = lax.dynamic_index_in_dim(far_types, slot_index, 1, False)
        onehot_source = (parent_ids[:, None] == source_ids[None, :]).astype(jnp.float32)
        chosen = jnp.einsum("sjq,qp->sjp", sources, onehot_source, precision=HIGHEST)
        onehot_kind = (type_ids[None, :] == kind_ids[:, None]).astype(jnp.float32)
        factor = jnp.einsum("stk,tp->skp", translate, onehot_kind, precision=HIGHEST)
        real_part = factor[0] * chosen[0] - factor[1] * chosen[1]
        imag_part = factor[0] * chosen[1] + factor[1] * chosen[0]
        return total + jnp.stack([real_part, imag_part])

    incoming = lax.fori_loop(0, list_len, add_entry, jnp.zeros(parents.shape, jnp.float32))
    returned = lax.all_to_all(incoming, "ang", split_axis=2, concat_axis=1, tiled=True)
    child_in = spread(returned, cosine, sine_part)
    leaf_in = jnp.einsum("jk,sjc->skc", interp, child_in, precision=HIGHEST)
    far_part = complex_product("kn,kc->cn", receive, leaf_in)
    return far_part + near_part


def solution(mesh):
    in_specs = (
        P(None, ("grp", "ang"), None),
        P(("grp", "ang"), None, None, None),
        P(("grp", "ang")),
        P(("grp", "ang")),
        P(),
        P(),
        P(),
        P(),
        P(None, None, "ang"),
        P("grp", None),
        P("grp", None),
    )
    out_specs = P(None, ("grp", "ang"), None)
    return jax.shard_map(
        on_device, mesh=mesh, in_specs=in_specs, out_specs=out_specs, check_vma=False
    )
```

profile of v0, /device:TPU:0, one launch (start us, length us, event | category | flops | bytes accessed | tf_op | source)
XLA Modules:
  0.0 137.0 jit_solution(7326102560977606023)
XLA Ops:
  6.5 2.0 %fusion.52 = f32[1024,128]{1,0:T(8,128)S(1)} fusion(f32[2,1024,256]{2,1,0:T(8,128)} %param.17, bf16[2,128,256]{2,1,0:T(8,128)(2,1)} %param.13), kind=kOutput, calls=%fused_computation.57 | convolution fusion | flops 402653184 | bytes 1638400 | tf_op jit(solution)/shard_map/kn,cn->kc/dot_general | solution.py:13
  8.5 2.1 %fusion.54 = f32[1024,128]{1,0:T(8,128)S(1)} fusion(f32[2,1024,256]{2,1,0:T(8,128)} %param.17, bf16[2,128,256]{2,1,0:T(8,128)(2,1)} %param.13), kind=kOutput, calls=%fused_computation.59 | convolution fusion | flops 402653184 | bytes 1638400 | tf_op jit(solution)/shard_map/kn,cn->kc/dot_general | solution.py:10
  10.8 1.8 %fusion.36 = f32[1,1024,128]{2,1,0:T(8,128)S(1)} fusion(f32[1024,128]{1,0:T(8,128)S(1)} %fusion.52, f32[2,1024,256]{2,1,0:T(8,128)} %param.17, bf16[2,128,256]{2,1,0:T(8,128)(2,1)S(1)} %copy-done.3), kind=kOutput, calls=%fused_computation.37 | convolution fusion | flops 402784256 | bytes 2162688 | tf_op jit(solution)/shard_map/kn,cn->kc/dot_general | solution.py:13
  12.6 1.8 %fusion.37 = f32[1,1024,128]{2,1,0:T(8,128)S(1)} fusion(f32[1024,128]{1,0:T(8,128)S(1)} %fusion.54, f32[2,1024,256]{2,1,0:T(8,128)} %param.17, bf16[2,128,256]{2,1,0:T(8,128)(2,1)S(1)} %copy-done.3), kind=kOutput, calls=%fused_computation.39 | convolution fusion | flops 402784256 | bytes 2162688 | tf_op jit(solution)/shard_map/kn,cn->kc/dot_general | solution.py:10
  14.5 10.7 %fusion.25 = f32[2,1536,128]{1,2,0:T(8,128)S(1)} fusion(f32[1536,1024]{1,0:T(8,128)S(1)} %copy-done, f32[1,1024,128]{2,1,0:T(8,128)S(1)} %fusion.36, f32[1,1024,128]{2,1,0:T(8,128)S(1)} %fusion.37), kind=kOutput, calls=%fused_computation.31 | convolution fusion | flops 4832100352 | bytes 8912896 | tf_op jit(solution)/shard_map/jk,skc->sjc/dot_general | solution.py:75
  26.6 2.8 %reshape.159 = f32[8,1,6144]{2,1,0:T(1,128)} reshape(f32[1536,2,16]{2,1,0:T(2,128)S(1)} %bitcast.177) | data formatting | bytes 393216
  29.4 7.3 %all-to-all-start = ((f32[8,1,6144]{2,1,0:T(1,128)}), f32[8,1,6144]{2,1,0:T(1,128)S(1)}, u32[]{:S(2)}, u32[]{:S(2)}) async-start(f32[8,1,6144]{2,1,0:T(1,128)} %reshape.159), calls=%async_computation | async-start | bytes 393216 | tf_op jit(solution)/shard_map/all_to_all | solution.py:77
  36.7 0.8 copy.49
  37.5 7.1 %all-to-all-done = f32[8,1,6144]{2,1,0:T(1,128)S(1)} async-done(((f32[8,1,6144]{2,1,0:T(1,128)}), f32[8,1,6144]{2,1,0:T(1,128)S(1)}, u32[]{:S(2)}, u32[]{:S(2)}) %all-to-all-start) | async-done | bytes 196640 | tf_op jit(solution)/shard_map/all_to_all | solution.py:77
  45.1 1.1 reduce
  46.2 2.1 %reshape.160 = f32[1536,2,16]{2,1,0:T(2,128)S(1)} reshape(f32[8,6144]{1,0:T(8,128)S(1)} %reduce) | data formatting | bytes 393216
  48.3 1.5 %copy.60 = f32[2,8,192,16]{2,3,1,0:T(8,128)S(1)} copy(f32[2,8,192,16]{3,0,2,1:T(2,128)S(1)} %bitcast.178) | data formatting | bytes 393216 | tf_op jit(solution)/shard_map/all_to_all | solution.py:77
  49.8 10.0 %all_gather.6 = f32[2,192,512]{1,2,0:T(8,128)S(1)} all-gather(f32[2,192,128]{1,2,0:T(8,128)S(1)} %bitcast.179), channel_id=1, replica_groups=mesh['grp'=4,'ang'=8] {'grp'}, dimensions={2}, use_global_device_ids=true | all-gather | bytes 983040 | tf_op jit(solution)/shard_map/all_gather | solution.py:78
  60.2 27.9 %while.14 = (s32[]{:T(128)}, f32[2,192,128]{2,1,0:T(8,128)S(1)}, s32[128,16]{0,1:T(8,128)}, f32[2,316,192]{1,2,0:T(8,128)S(1)}, s32[128,16]{0,1:T(8,128)}, /*index=5*/f32[2,192,512]{2,1,0:T(8,128)S(1)}, s32[]{:T(128)}, s32[]{:T(128)}) while((s32[]{:T(128)}, f32[2,192,128]{2,1,0:T(8,128)S(1)}, s32[128,16]{0,1:T(8,128)}, ...), condition=%wide.region_3.4_spmd.clone, body=%wide.region_2.3_spmd.clone.sunk | while | flops 488775168 | bytes 2847843 | solution.py:94
  88.1 0.8 copy.45
  89.0 3.6 %all-to-all-start.1 = ((f32[2,192,128]{1,0,2:T(2,128)}), f32[2,192,128]{1,0,2:T(2,128)S(1)}, u32[]{:S(2)}, u32[]{:S(2)}) async-start(f32[2,192,128]{1,0,2:T(2,128)} %copy.45), calls=%async_computation.1 | async-start | bytes 524288 | tf_op jit(solution)/shard_map/all_to_all | solution.py:95
  92.7 9.4 %all-to-all-done.1 = f32[2,192,128]{1,0,2:T(2,128)S(1)} async-done(((f32[2,192,128]{1,0,2:T(2,128)}), f32[2,192,128]{1,0,2:T(2,128)S(1)}, u32[]{:S(2)}, u32[]{:S(2)}) %all-to-all-start.1) | async-done | bytes 196640 | tf_op jit(solution)/shard_map/all_to_all | solution.py:95
  102.7 8.0 %fusion.31 = f32[2,1024,128]{1,2,0:T(8,128)S(1)} fusion(f32[1536,1024]{1,0:T(8,128)} %param.19, f32[1,1536,128]{1,2,0:T(8,128)S(1)} %get-tuple-element.213, f32[1,1536,128]{1,2,0:T(8,128)S(1)} %get-tuple-element.212), kind=kOutput, calls=%fused_computation.35 | convolution fusion | flops 4832231424 | bytes 8912896 | tf_op jit(solution)/shard_map/jk,sjc->skc/dot_general | solution.py:97
  113.3 1.9 %gather_fusion = bf16[40,2,256]{2,1,0:T(2,128)(2,1)S(1)} fusion(bf16[2,1024,256]{2,0,1:T(2,128)(2,1)} %all-gather.2.cloned.1.call-done, s32[1024]{0:T(1024)S(1)} %pad_clamp_fusion), kind=kCustom, calls=%fused_computation | custom fusion | bytes 82080 | tf_op jit(solution)/shard_map/jit(_take)/gather | solution.py:56
  115.4 4.1 %fusion.13 = f32[40,1,256]{2,1,0:T(1,128)S(1)} fusion(bf16[40,2,256,256]{3,2,1,0:T(8,128)(2,1)} %param.14, bf16[2,40,256]{2,0,1:T(2,128)(2,1)S(1)} %fusion.77), kind=kOutput, calls=%fused_computation.19 | convolution fusion | flops 5242880 | bytes 5324800 | tf_op jit(solution)/shard_map/bmn,bn->bm/dot_general | solution.py:64
  119.5 4.1 %fusion.15 = f32[40,1,256]{2,1,0:T(1,128)S(1)} fusion(bf16[40,2,256,256]{3,2,1,0:T(8,128)(2,1)} %param.14, bf16[2,40,256]{2,0,1:T(2,128)(2,1)S(1)} %fusion.77), kind=kOutput, calls=%fused_computation.21 | convolution fusion | flops 5242880 | bytes 5324800 | tf_op jit(solution)/shard_map/bmn,bn->bm/dot_general | solution.py:61
  123.6 4.0 %fusion.17 = f32[40,1,256]{2,1,0:T(1,128)S(1)} fusion(bf16[40,2,256,256]{3,2,1,0:T(8,128)(2,1)} %param.14, bf16[2,40,256]{2,0,1:T(2,128)(2,1)S(1)} %fusion.77), kind=kOutput, calls=%fused_computation.23 | convolution fusion | flops 5242880 | bytes 5324800 | tf_op jit(solution)/shard_map/bmn,bn->bm/dot_general | solution.py:62
  127.6 1.4 %fusion.19 = f32[40,1,256]{2,1,0:T(1,128)S(1)} fusion(bf16[40,2,256,256]{3,2,1,0:T(8,128)(2,1)S(1)} %bitcast.176, bf16[2,40,256]{2,0,1:T(2,128)(2,1)S(1)} %fusion.77), kind=kOutput, calls=%fused_computation.25 | convolution fusion | flops 5242880 | bytes 5324800 | tf_op jit(solution)/shard_map/bmn,bn->bm/dot_general | solution.py:59
  129.0 1.1 fusion.38
  (127 shorter events, 33.1 us)
Async XLA Ops:
  6.5 4.3 %copy-start.3 = (bf16[2,128,256]{2,1,0:T(8,128)(2,1)S(1)}, bf16[2,128,256]{2,1,0:T(8,128)(2,1)}, u32[]{:S(2)}) copy-start(bf16[2,128,256]{2,1,0:T(8,128)(2,1)} %param.13) | copy-start | bytes 393220
  6.5 4.1 %copy-start.4 = (f32[8,1536]{1,0:T(8,128)S(1)}, f32[8,1536]{1,0:T(8,128)}, u32[]{:S(2)}) copy-start(f32[8,1536]{1,0:T(8,128)} %param.20) | copy-start | bytes 147460
  6.5 7.9 %copy-start = (f32[1536,1024]{1,0:T(8,128)S(1)}, f32[1536,1024]{1,0:T(8,128)}, u32[]{:S(2)}) copy-start(f32[1536,1024]{1,0:T(8,128)} %param.19) | copy-start | bytes 18874372
  29.4 15.2 %all-to-all-start = ((f32[8,1,6144]{2,1,0:T(1,128)}), f32[8,1,6144]{2,1,0:T(1,128)S(1)}, u32[]{:S(2)}, u32[]{:S(2)}) async-start(f32[8,1,6144]{2,1,0:T(1,128)} %reshape.159), calls=%async_computation | async-start | bytes 393216 | tf_op jit(solution)/shard_map/all_to_all | solution.py:77
  36.6 76.7 %all-gather.2.cloned.1.call-start = ((), (), s32[]{:S(2)}) async-start(), calls=%async_computation.2 | async-start | bytes 1179648 | tf_op jit(solution)/shard_map/all_gather | solution.py:55
  48.3 11.9 %copy-start.1 = (f32[2,316,192]{1,2,0:T(8,128)S(1)}, f32[2,316,192]{1,2,0:T(8,128)}, u32[]{:S(2)}) copy-start(f32[2,316,192]{1,2,0:T(8,128)} %param.21) | copy-start | bytes 1456132
  60.2 32.4 %copy-start.6 = (s32[40]{0:T(128)S(1)}, s32[40]{0:T(128)}, u32[]{:S(2)}) copy-start(s32[40]{0:T(128)} %param.16) | copy-start | bytes 484
  89.0 13.1 %all-to-all-start.1 = ((f32[2,192,128]{1,0,2:T(2,128)}), f32[2,192,128]{1,0,2:T(2,128)S(1)}, u32[]{:S(2)}, u32[]{:S(2)}) async-start(f32[2,192,128]{1,0,2:T(2,128)} %copy.45), calls=%async_computation.1 | async-start | bytes 524288 | tf_op jit(solution)/shard_map/all_to_all | solution.py:95
  102.7 8.0 %copy-start.2 = (f32[2,1024,256]{2,1,0:T(8,128)S(1)}, f32[2,1024,256]{2,1,0:T(8,128)}, u32[]{:S(2)}) copy-start(f32[2,1024,256]{2,1,0:T(8,128)} %param.18) | copy-start | bytes 6291460
  112.0 15.5 %slice-start = ((s8[10485760]{0:T(1024)(128)(4,1)}), s8[2097152]{0:T(1024)(128)(4,1)S(1)}, s32[]{:S(2)}) async-start(s8[10485760]{0:T(1024)(128)(4,1)} %bitcast.175), calls=%async_computation.3 | async-start | bytes 4194304
  115.3 12.2 %slice-start.1 = ((s8[10485760]{0:T(1024)(128)(4,1)}), s8[4194304]{0:T(1024)(128)(4,1)S(1)}, s32[]{:S(2)}) async-start(s8[10485760]{0:T(1024)(128)(4,1)} %bitcast.175), calls=%async_computation.4 | async-start | bytes 8388608
  119.5 8.1 %slice-start.2 = ((s8[10485760]{0:T(1024)(128)(4,1)}), s8[4194304]{0:T(1024)(128)(4,1)S(1)}, s32[]{:S(2)}) async-start(s8[10485760]{0:T(1024)(128)(4,1)} %bitcast.175), calls=%async_computation.5 | async-start | bytes 8388608
  127.5 1.5 %copy-start.5 = (s32[40]{0:T(128)S(1)}, s32[40]{0:T(128)}, u32[]{:S(2)}) copy-start(s32[40]{0:T(128)} %param.15) | copy-start | bytes 484
Sparse Core Ops, SparseCore 0:
  39.6 41.4 all-gather.1
where the time goes:
time: 138 us; the launch traced here: 137 us
  matrix products  58.1 us (42%)
  local copies, waits for them, and re-layouts  23.6 us (17%)
  waiting for transfers between devices  16.5 us (12%)
  between operations  13.8 us (10%)
  starting transfers between devices  10.9 us (8%)
  blocking collectives  10 us (7%)
  other arithmetic  3.34 us (2%)
    eq x16, local copies, waits for them, and re-layouts, add_entry(): parent_ids[:, None] == source_ids[None, :]  11.4 us
    dot_general x1, matrix products, on_device(): children = jnp.einsum('jk,skc->sjc', interp, radiated, precision=HIGHEST)  10.7 us
    all_gather x1, blocking collectives, on_device(): sources = lax.all_gather(parents, 'grp', axis=2, tiled=True)  10 us
    all_to_all x1, waiting for transfers between devices, on_device(): lax.all_to_all(incoming, 'ang', split_axis=2, concat_axis=1, tiled=True)  9.39 us
    dot_general x16, matrix products, add_entry(): jnp.einsum('sjq,qp->sjp', sources, onehot_source, precision=HIGHEST)  8.17 us
    dot_general x1, matrix products, on_device(): leaf_in = jnp.einsum('jk,sjc->skc', interp, child_in, precision=HIGHEST)  7.97 us
    all_to_all x1, starting transfers between devices, on_device(): lax.all_to_all(own_parents, 'ang', split_axis=1, concat_axis=2, tiled=True)  7.28 us
    all_to_all x1, waiting for transfers between devices, on_device(): lax.all_to_all(own_parents, 'ang', split_axis=1, concat_axis=2, tiled=True)  7.08 us
  transfers between devices with their start and end apart: 3, of which 2 were waited for; matrix products, arithmetic and copies ran while one was open for 33% of the time, Pallas kernels for 0%

commit v1 on v0

v1 whole, which is shorter than its diff:
```python
import functools
import jax
import jax.numpy as jnp
from jax import lax
from jax.experimental import pallas as pl
from jax.experimental.pallas import tpu as pltpu
from jax.sharding import PartitionSpec as P

F32 = jnp.float32
BF16 = jnp.bfloat16
VMEM_LIMIT = 48 << 20


def halves(x):
    high = x.astype(BF16)
    return high, (x - high.astype(F32)).astype(BF16)


def dot_nt(a, b):
    return lax.dot_general(a, b, (((1,), (1,)), ((), ())), preferred_element_type=F32)


def dot_nn(a, b):
    return lax.dot_general(a, b, (((1,), (0,)), ((), ())), preferred_element_type=F32)


def iota(shape, dim):
    return lax.broadcasted_iota(jnp.int32, shape, dim)


class Layout:
    def __init__(self, n_grp, n_ang, k_up, list_len):
        self.n_grp, self.n_ang = n_grp, n_ang
        self.n_dev = n_grp * n_ang
        self.own = k_up // self.n_dev
        self.pad = -(-self.own // 8) * 8
        self.lists = 2 * self.pad
        self.list_len = list_len

    def first(self, dest):
        grp, ang = divmod(dest, self.n_ang)
        return (ang * self.n_grp + grp) * self.own


def forward_kernel(lay, cur_ref, rad_ref, interp_ref, cos_ref, sin_ref, lists_ref, out_ref,
                   high_ref, low_ref, par_ref):
    step = pl.program_id(0)
    count = cur_ref.shape[1]
    n_par = count // 8

    @pl.when(step == 0)
    def _():
        row = iota((count, count), 0)
        col = iota((count, count), 1)
        order = (col == (row % n_par) * 8 + row // n_par).astype(BF16)
        cur_re = dot_nn(order, cur_ref[0]).astype(BF16)
        cur_im = dot_nn(order, cur_ref[1]).astype(BF16)
        left = jnp.concatenate([cur_re, cur_im], axis=0)
        right = jnp.concatenate([-cur_im, cur_re], axis=0)
        k_leaf = rad_ref.shape[1]
        width = 256
        for k in range(0, k_leaf, width):
            rr_high, rr_low = halves(rad_ref[0, k:k + width, :])
            ri_high, ri_low = halves(rad_ref[1, k:k + width, :])
            radiated = (dot_nt(left, rr_high) + dot_nt(left, rr_low)
                        + dot_nt(right, ri_high) + dot_nt(right, ri_low))
            high, low = halves(radiated)
            high_ref[:, k:k + width] = high
            low_ref[:, k:k + width] = low

    in_high, in_low = halves(interp_ref[...])
    children = dot_nt(high_ref[...], in_high) + dot_nt(high_ref[...], in_low) + dot_nt(low_ref[...], in_high)
    re_sum = im_sum = None
    for t in range(8):
        c = cos_ref[t:t + 1, :]
        s = sin_ref[t:t + 1, :]
        re = children[t * n_par:(t + 1) * n_par]
        im = children[count + t * n_par:count + (t + 1) * n_par]
        re_t = c * re - s * im
        im_t = c * im + s * re
        re_sum = re_t if t == 0 else re_sum + re_t
        im_sum = im_t if t == 0 else im_sum + im_t
    width = interp_ref.shape[0]
    at = pl.ds(pl.multiple_of(step * width, width), width)
    par_ref[0, :, at] = re_sum
    par_ref[1, :, at] = im_sum

    @pl.when(step == pl.num_programs(0) - 1)
    def _():
        out_ref[...] = jnp.zeros_like(out_ref)
        for dest in range(lay.n_dev):
            j = lay.first(dest)
            out_ref[dest, :, 0:lay.own] = par_ref[0, :, j:j + lay.own]
            out_ref[dest, :, lay.pad:lay.pad + lay.own] = par_ref[1, :, j:j + lay.own]
            out_ref[dest, :, lay.lists:lay.lists + lay.list_len] = lists_ref[...]


def forward(lay, current, radiate, interp, cosine, sine, lists):
    count, unk = current.shape[1:]
    k_leaf = radiate.shape[1]
    k_up = interp.shape[0]
    width = 256
    n_par = count // 8
    whole = lambda *shape: pl.BlockSpec(shape, lambda i: (0,) * len(shape))
    return pl.pallas_call(
        functools.partial(forward_kernel, lay),
        grid=(k_up // width,),
        in_specs=[
            whole(2, count, unk),
            whole(2, k_leaf, unk),
            pl.BlockSpec((width, k_leaf), lambda i: (i, 0)),
            pl.BlockSpec((8, width), lambda i: (0, i)),
            pl.BlockSpec((8, width), lambda i: (0, i)),
            whole(n_par, lay.list_len),
        ],
        out_specs=whole(lay.n_dev, n_par, 128),
        out_shape=jax.ShapeDtypeStruct((lay.n_dev, n_par, 128), F32),
        scratch_shapes=[
            pltpu.VMEM((2 * count, k_leaf), BF16),
            pltpu.VMEM((2 * count, k_leaf), BF16),
            pltpu.VMEM((2, n_par, k_up), F32),
        ],
        compiler_params=pltpu.CompilerParams(vmem_limit_bytes=VMEM_LIMIT),
        cost_estimate=pl.CostEstimate(flops=3 * 10**9, bytes_accessed=9 * 10**6, transcendentals=0),
        name="forward",
    )(current, radiate, interp, cosine, sine, lists)


def translate_kernel(lay, n_kind, got_ref, table_ref, out_ref, x_ref, t_ref, acc_ref):
    n_par = got_ref.shape[0]
    span = 2 * lay.pad
    n_pad = table_ref.shape[1]
    got = got_ref[...].T
    high, low = halves(got[0:span])
    x_ref[0:span] = high
    x_ref[span:2 * span] = low
    high, low = halves(table_ref[...])
    t_ref[0:span] = high
    t_ref[span:2 * span] = low
    codes = got[lay.lists:lay.lists + lay.list_len].astype(jnp.int32)
    width = min(512, n_par)
    rows_src = iota((n_par, width), 0)
    rows_kind = iota((n_pad, width), 0)
    for p in range(0, n_par, width):
        re_sum = im_sum = None
        for m in range(lay.list_len):
            code = codes[m:m + 1, p:p + width]
            source = jnp.right_shift(code, 9)
            kind = jnp.bitwise_and(code, 511)
            pick = (rows_src == source).astype(BF16)
            both = dot_nn(x_ref[...], pick)
            chosen = both[0:span] + both[span:2 * span]
            pick = (rows_kind == kind).astype(BF16)
            both = dot_nn(t_ref[...], pick)
            factor = both[0:span] + both[span:2 * span]
            fr, fi = factor[0:lay.pad], factor[lay.pad:span]
            cr, ci = chosen[0:lay.pad], chosen[lay.pad:span]
            re = fr * cr - fi * ci
            im = fr * ci + fi * cr
            re_sum = re if m == 0 else re_sum + re
            im_sum = im if m == 0 else im_sum + im
        acc_ref[0:lay.pad, p:p + width] = re_sum
        acc_ref[lay.pad:span, p:p + width] = im_sum
    acc_ref[span:128] = jnp.zeros((128 - span, n_par), F32)
    out_ref[...] = acc_ref[...].T


def translate_far(lay, got, table, n_kind):
    n_par = got.shape[0]
    span = 2 * lay.pad
    return pl.pallas_call(
        functools.partial(translate_kernel, lay, n_kind),
        out_shape=jax.ShapeDtypeStruct((n_par, 128), F32),
        scratch_shapes=[
            pltpu.VMEM((2 * span, n_par), BF16),
            pltpu.VMEM((2 * span, table.shape[1]), BF16),
            pltpu.VMEM((128, n_par), F32),
        ],
        compiler_params=pltpu.CompilerParams(vmem_limit_bytes=VMEM_LIMIT),
        cost_estimate=pl.CostEstimate(flops=4 * 10**9, bytes_accessed=10**6, transcendentals=0),
        name="translate_far",
    )(got, table)


def backward_kernel(lay, got_ref, interp_ref, rec_ref, cos_ref, sin_ref, near_ref, out_ref,
                    inc_ref, high_ref, low_ref):
    step = pl.program_id(0)
    n_par = got_ref.shape[1]
    count = 8 * n_par

    @pl.when(step == 0)
    def _():
        for dest in range(lay.n_dev):
            j = lay.first(dest)
            inc_ref[0, :, j:j + lay.own] = got_ref[dest, :, 0:lay.own]
            inc_ref[1, :, j:j + lay.own] = got_ref[dest, :, lay.pad:lay.pad + lay.own]
        c = cos_ref[...]
        s = sin_ref[...]
        for p in range(0, n_par, 2):
            res, ims = [], []
            for q in (p, p + 1):
                re = inc_ref[0, q:q + 1, :]
                im = inc_ref[1, q:q + 1, :]
                res.append(c * re + s * im)
                ims.append(c * im - s * re)
            high, low = halves(jnp.concatenate(res, axis=0))
            high_ref[8 * p:8 * p + 16] = high
            low_ref[8 * p:8 * p + 16] = low
            high, low = halves(jnp.concatenate(ims, axis=0))
            high_ref[count + 8 * p:count + 8 * p + 16] = high
            low_ref[count + 8 * p:count + 8 * p + 16] = low
        out_ref[...] = near_ref[...]

    in_high, in_low = halves(interp_ref[...])
    leaf = dot_nn(high_ref[...], in_high) + dot_nn(high_ref[...], in_low) + dot_nn(low_ref[...], in_high)
    leaf_high, leaf_low = halves(leaf)
    rr_high, rr_low = halves(rec_ref[0])
    ri_high, ri_low = halves(rec_ref[1])
    by_re = dot_nn(leaf_high, rr_high) + dot_nn(leaf_high, rr_low) + dot_nn(leaf_low, rr_high)
    by_im = dot_nn(leaf_high, ri_high) + dot_nn(leaf_high, ri_low) + dot_nn(leaf_low, ri_high)
    out_ref[0] += by_re[0:count] - by_im[count:2 * count]
    out_ref[1] += by_im[0:count] + by_re[count:2 * count]


def backward(lay, got, interp, receive, cosine, sine, near):
    n_par = got.shape[1]
    count = 8 * n_par
    k_up, k_leaf = interp.shape
    unk = receive.shape[2]
    width = 256
    whole = lambda *shape: pl.BlockSpec(shape, lambda i: (0,) * len(shape))
    return pl.pallas_call(
        functools.partial(backward_kernel, lay),
        grid=(k_leaf // width,),
        in_specs=[
            whole(lay.n_dev, n_par, 128),
            pl.BlockSpec((k_up, width), lambda i: (0, i)),
            pl.BlockSpec((2, width, unk), lambda i: (0, i, 0)),
            whole(8, k_up),
            whole(8, k_up),
            whole(2, count, unk),
        ],
        out_specs=whole(2, count, unk),
        out_shape=jax.ShapeDtypeStruct((2, count, unk), F32),
        scratch_shapes=[
            pltpu.VMEM((2, n_par, k_up), F32),
            pltpu.VMEM((2 * count, k_up), BF16),
            pltpu.VMEM((2 * count, k_up), BF16),
        ],
        compiler_params=pltpu.CompilerParams(vmem_limit_bytes=VMEM_LIMIT),
        cost_estimate=pl.CostEstimate(flops=3 * 10**9, bytes_accessed=9 * 10**6, transcendentals=0),
        name="backward",
    )(got, interp, receive, cosine, sine, near)


def near_kernel(n_block, cols_ref, rows_ref, cur_ref, blocks_ref, out_ref, pick_ref, own_ref):
    step = pl.program_id(0)
    here = blocks_ref.shape[0]
    unk = blocks_ref.shape[2]
    slots, _, group, _ = cur_ref.shape

    @pl.when(step == 0)
    def _():
        col = cols_ref[...]
        for part in range(2):
            total = jnp.zeros((64, unk), F32)
            for slot in range(slots):
                mark = (iota((64, group), 1) + slot * group == col).astype(BF16)
                total = total + dot_nn(mark, cur_ref[slot, part])
            pick_ref[64 * part:64 * part + 64] = total.astype(BF16)
        own_ref[...] = jnp.zeros_like(own_ref)

    lane = iota((2 * unk, 128), 1) % 64
    own = own_ref[...]
    for i in range(here):
        block = blocks_ref[i].reshape(2 * unk, unk)
        own = jnp.where(lane == step * here + i, dot_nt(block, pick_ref[...]), own)
    own_ref[...] = own

    @pl.when(step == pl.num_programs(0) - 1)
    def _():
        by_block = own_ref[...].T
        by_re, by_im = by_block[:, 0:unk], by_block[:, unk:2 * unk]
        re = by_re[0:64] - by_im[64:128]
        im = by_re[64:128] + by_im[0:64]
        count = out_ref.shape[1]
        mark = (iota((count, 64), 0) == rows_ref[...]).astype(BF16)
        for part, value in ((0, re), (1, im)):
            high, low = halves(value)
            out_ref[part] = dot_nn(mark, high) + dot_nn(mark, low)


def near_field(cols, rows, gathered, blocks, count):
    n_block, _, unk, _ = blocks.shape
    here = 8
    whole = lambda *shape: pl.BlockSpec(shape, lambda i: (0,) * len(shape))
    return pl.pallas_call(
        functools.partial(near_kernel, n_block),
        grid=(n_block // here,),
        in_specs=[
            whole(64, 1),
            whole(1, 64),
            whole(*gathered.shape),
            pl.BlockSpec((here, 2, unk, unk), lambda i: (i, 0, 0, 0)),
        ],
        out_specs=whole(2, count, unk),
        out_shape=jax.ShapeDtypeStruct((2, count, unk), F32),
        scratch_shapes=[
            pltpu.VMEM((128, unk), BF16),
            pltpu.VMEM((2 * unk, 128), F32),
        ],
        compiler_params=pltpu.CompilerParams(vmem_limit_bytes=VMEM_LIMIT),
        cost_estimate=pl.CostEstimate(flops=2 * 10**9, bytes_accessed=12 * 10**6, transcendentals=0),
        name="near_field",
    )(cols, rows, gathered, blocks)


def on_device(n_grp, n_ang, current, near_blocks, near_rows, near_cols, radiate, receive, interp,
              shift_phase, translate, far_sources, far_types):
    count, unk = current.shape[1:]
    n_par = count // 8
    n_block = near_blocks.shape[0]
    k_up = interp.shape[0]
    n_kind = translate.shape[1]
    lay = Layout(n_grp, n_ang, k_up, far_sources.shape[1])
    grp = lax.axis_index("grp")
    ang = lax.axis_index("ang")
    axes = ("grp", "ang")

    swapped = lax.ppermute(current, "ang", [(i, i ^ 1) for i in range(n_ang)])
    pair = jnp.concatenate([current, swapped], axis=1)
    sides = [[i for i in range(n_ang) if i % 2 == side] for side in range(2)]
    gathered = lax.all_gather(pair, "ang", axis_index_groups=sides)

    cosine = jnp.cos(shift_phase)
    sine = jnp.sin(shift_phase)
    own_src = lax.dynamic_slice_in_dim(far_sources, ang * n_par, n_par, 0)
    own_kind = lax.dynamic_slice_in_dim(far_types, ang * n_par, n_par, 0)
    lists = (own_src * 512 + own_kind).astype(F32)

    message = forward(lay, current, radiate, interp, cosine, sine, lists)
    got = lax.all_to_all(message, axes, 0, 0)

    table = lax.dynamic_slice_in_dim(translate, grp * lay.own, lay.own, 2)
    kind_pad = -(-n_kind // 128) * 128
    table = jnp.pad(table, ((0, 0), (0, kind_pad - n_kind), (0, lay.pad - lay.own)))
    table = jnp.transpose(table, (0, 2, 1)).reshape(2 * lay.pad, kind_pad)

    incoming = translate_far(lay, got.reshape(lay.n_dev * n_par, 128), table, n_kind)
    returned = lax.all_to_all(incoming.reshape(lay.n_dev, n_par, 128), axes, 0, 0)

    owner = near_cols // count
    place = (owner // 2) * 2 * count + ((owner % 2) ^ (ang % 2)) * count + near_cols % count
    cols = jnp.full((64, 1), -1, jnp.int32).at[:n_block, 0].set(place)
    rows = jnp.full((1, 64), -1, jnp.int32).at[0, :n_block].set(near_rows)
    near = near_field(cols, rows, gathered, near_blocks, count)

    return backward(lay, returned, interp, receive, cosine, sine, near)


def solution(mesh):
    both = ("grp", "ang")
    in_specs = (
        P(None, both, None),
        P(both, None, None, None),
        P(both),
        P(both),
        P(),
        P(),
        P(),
        P(),
        P(None, None, "ang"),
        P("grp", None),
        P("grp", None),
    )
    run = functools.partial(on_device, mesh.shape["grp"], mesh.shape["ang"])
    return jax.shard_map(run, mesh=mesh, in_specs=in_specs, out_specs=P(None, both, None), check_vma=False)
```

time: 138 us -> 84 us (0.61)
  matrix products: 58.1 us -> 0 us
  Pallas kernels: 0 us -> 29.3 us
  local copies, waits for them, and re-layouts: 23.6 us -> 5.77 us
  blocking collectives: 10 us -> 0 us
  waiting for transfers between devices: 16.5 us -> 20.2 us
    dot_general x31 -> x0, matrix products: 51.8 us -> none  [the longest x1 10.7 us: on_device(): children = jnp.einsum('jk,skc->sjc', interp, radiated, precision=HIGHEST)]
    pallas_call x0 -> x4, Pallas kernels: none -> 29.3 us  [the longest x1 8.59 us: backward(): pl.pallas_call(functools.partial(backward_kernel, lay), grid=(k_leaf // w...]
    eq x16 -> x0, local copies, waits for them, and re-layouts: 11.4 us -> none  [add_entry(): parent_ids[:, None] == source_ids[None, :]]
    all_gather x1 -> x0, blocking collectives: 10 us -> none  [on_device(): sources = lax.all_gather(parents, 'grp', axis=2, tiled=True)]
    while x16 -> x0, matrix products: 6.35 us -> none
    ppermute x0 -> x1, starting transfers between devices: none -> 2.97 us  [on_device(): swapped = lax.ppermute(current, 'ang', [(i, i ^ 1) for i in range(n_ang)])]
    all_to_all x2, starting transfers between devices: 10.9 us -> 8.68 us  [the longest x1 6.09 us: on_device(): got = lax.all_to_all(message, axes, 0, 0)]
    unnamed x24 -> x16, local copies, waits for them, and re-layouts: 6.08 us -> 3.86 us
  transfers between devices with their start and end apart: 3 -> 4, of which waited for: 2 -> 3; matrix products, arithmetic and copies ran while one was open for 33% -> 4% of each run, Pallas kernels for 0% -> 25%
where the time goes in v1:
time: 84 us; the launch traced here: 83.4 us
  Pallas kernels  29.3 us (35%)
  waiting for transfers between devices  20.2 us (24%)
  between operations  13.5 us (16%)
  starting transfers between devices  11.6 us (14%)
  local copies, waits for them, and re-layouts  5.77 us (7%)
  other arithmetic  2.86 us (3%)
    all_to_all x1, waiting for transfers between devices, on_device(): got = lax.all_to_all(message, axes, 0, 0)  18 us
    pallas_call x1, Pallas kernels, backward(): pl.pallas_call(functools.partial(backward_kernel, lay), grid=(k_leaf // w...  8.59 us
    pallas_call x1, Pallas kernels, forward(): pl.pallas_call(functools.partial(forward_kernel, lay), grid=(k_up // widt...  8.24 us
    pallas_call x1, Pallas kernels, near_field(): pl.pallas_call(functools.partial(near_kernel, n_block), grid=(n_block //...  7.64 us
    all_to_all x1, starting transfers between devices, on_device(): got = lax.all_to_all(message, axes, 0, 0)  6.09 us
    pallas_call x1, Pallas kernels, translate_far(): pl.pallas_call(functools.partial(translate_kernel, lay, n_kind), out_shap...  4.86 us
    unnamed x16, local copies, waits for them, and re-layouts  3.86 us
    ppermute x1, starting transfers between devices, on_device(): swapped = lax.ppermute(current, 'ang', [(i, i ^ 1) for i in range(n_ang)])  2.97 us
  transfers between devices with their start and end apart: 4, of which 3 were waited for; matrix products, arithmetic and copies ran while one was open for 4% of the time, Pallas kernels for 25%

profile of v1, /device:TPU:0, one launch (start us, length us, event | category | flops | bytes accessed | tf_op | source)
XLA Modules:
  0.0 83.4 jit_solution(13121929501226975482)
XLA Ops:
  6.5 3.0 %collective-permute-start = (bf16[2,128,256]{2,1,0:T(8,128)(2,1)}, bf16[2,128,256]{2,1,0:T(8,128)(2,1)S(1)}, u32[]{:S(2)}, u32[]{:S(2)}) collective-permute-start(bf16[2,128,256]{2,1,0:T(8,128)(2,1)} %cur_ref.1), channel_id=1, source_target_pairs={{0,1},{1,0},{2,3},{3,2},{4,5},{5,4},{6,7},{7,6},{8,9},{9,8},{10,11... | collective-permute-start | bytes 393224 | tf_op jit(solution)/shard_map/ppermute | solution.py:330
  9.5 0.8 constant_dynamic-slice_fusion.1
  10.3 0.1 copy.18
  10.4 0.1 copy.19
  10.4 1.0 %fusion.6 = (f32[8,1536]{1,0:T(8,128)S(1)}, f32[8,1536]{1,0:T(8,128)S(1)}) fusion(f32[8,1536]{1,0:T(8,128)} %param.22), kind=kLoop, calls=%fused_computation.23 | loop fusion | bytes 147456 | tf_op jit(solution)/shard_map/sin | solution.py:336
  11.4 1.8 %collective-permute-done = bf16[2,128,256]{2,1,0:T(8,128)(2,1)S(1)} collective-permute-done((bf16[2,128,256]{2,1,0:T(8,128)(2,1)}, bf16[2,128,256]{2,1,0:T(8,128)(2,1)S(1)}, u32[]{:S(2)}, u32[]{:S(2)}) %collective-permute-start) | collective-permute-done | bytes 131104 | tf_op jit(solution)/shard_map/ppermute | solution.py:330
  13.2 1.6 %pad_maximum_fusion = bf16[2,256,256]{2,1,0:T(8,128)(2,1)} fusion(bf16[2,128,256]{2,1,0:T(8,128)(2,1)S(1)} %collective-permute-done, bf16[2,128,256]{2,1,0:T(8,128)(2,1)} %cur_ref.1), kind=kLoop, calls=%fused_computation | loop fusion | flops 524288 | bytes 524288 | tf_op jit(solution)/shard_map/concatenate | solution.py:331
  14.9 0.0 all-gather.3.cloned.1.call-update
  14.9 0.0 copy-start.2
  14.9 0.9 %copy-done.2 = bf16[2,128,256]{2,1,0:T(8,128)(2,1)S(1)} copy-done((bf16[2,128,256]{2,1,0:T(8,128)(2,1)S(1)}, bf16[2,128,256]{2,1,0:T(8,128)(2,1)}, u32[]{:S(2)}) %copy-start.2) | copy-done | bytes 131096
  15.8 1.6 %copy-done.3 = f32[2,1024,256]{2,1,0:T(8,128)S(1)} copy-done((f32[2,1024,256]{2,1,0:T(8,128)S(1)}, f32[2,1024,256]{2,1,0:T(8,128)}, u32[]{:S(2)}) %copy-start.3) | copy-done | bytes 2097176
  17.4 8.2 %forward.1 = f32[32,16,128]{2,1,0:T(8,128)} custom-call(bf16[2,128,256]{2,1,0:T(8,128)(2,1)S(1)} %copy-done.2, f32[2,1024,256]{2,1,0:T(8,128)S(1)} %copy-done.3, f32[1536,1024]{1,0:T(8,128)} %interp_ref.3, f32[8,1536]{1,0:T(8,128)S(1)} %get-tuple-element.30.cos_ref, f32[8,1536]{1,0:T(8,128)S(1)} %get-tuple-element.29.sin_ref, ...), custom_call_target="tpu_custom_call" | custom-call | flops 3000000000 | bytes 9000000 | tf_op jit(solution)/shard_map/forward/pallas_call | solution.py:105
  25.6 6.1 %all-to-all-start = ((f32[32,16,128]{2,1,0:T(8,128)}), f32[32,16,128]{2,1,0:T(8,128)S(1)}, u32[]{:S(2)}, u32[]{:S(2)}) async-start(f32[32,16,128]{2,1,0:T(8,128)} %forward.1), calls=%async_computation | async-start | bytes 524288 | tf_op jit(solution)/shard_map/all_to_all | solution.py:342
  31.8 18.0 %all-to-all-done = f32[32,16,128]{2,1,0:T(8,128)S(1)} async-done(((f32[32,16,128]{2,1,0:T(8,128)}), f32[32,16,128]{2,1,0:T(8,128)S(1)}, u32[]{:S(2)}, u32[]{:S(2)}) %all-to-all-start) | async-done | bytes 262176 | tf_op jit(solution)/shard_map/all_to_all | solution.py:342
  49.8 4.9 %translate_far.1 = f32[512,128]{1,0:T(8,128)} custom-call(f32[512,128]{1,0:T(8,128)S(1)} %bitcast.11, f32[96,384]{1,0:T(8,128)S(1)} %bitcast.12), custom_call_target="tpu_custom_call" | custom-call | flops 4000000000 | bytes 1000000 | tf_op jit(solution)/shard_map/translate_far/pallas_call | solution.py:171
  54.7 2.6 %all-to-all-start.1 = ((f32[32,16,128]{2,1,0:T(8,128)}), f32[32,16,128]{2,1,0:T(8,128)S(1)}, u32[]{:S(2)}, u32[]{:S(2)}) async-start(f32[32,16,128]{2,1,0:T(8,128)} %bitcast.3), calls=%async_computation.1 | async-start | bytes 524288 | tf_op jit(solution)/shard_map/all_to_all | solution.py:350
  57.3 0.1 copy.17
  57.4 0.6 compare_reduce_fusion
  58.0 0.6 fusion.1
  58.6 0.0 all-gather.3.cloned.1.call-done
  58.7 1.2 %copy-done.1 = bf16[8,256,256]{2,1,0:T(8,128)(2,1)S(1)} copy-done((bf16[8,256,256]{2,1,0:T(8,128)(2,1)S(1)}, bf16[8,256,256]{2,1,0:T(8,128)(2,1)}, u32[]{:S(2)}) %copy-start.1) | copy-done | bytes 1048600
  59.9 7.6 %near_field.1.near_ref = f32[2,128,256]{2,1,0:T(8,128)S(1)} custom-call(s32[64,1]{1,0:T(8,128)S(1)} %scatter.6.cols_ref, s32[1,64]{1,0:T(1,128)S(1)} %scatter.9.rows_ref, bf16[4,2,256,256]{3,2,1,0:T(8,128)(2,1)S(1)} %bitcast.10, bf16[40,2,256,256]{3,2,1,0:T(8,128)(2,1)} %blocks_ref.1), custom_call_target="tpu_custom_call" | custom-call | flops 2000000000 | bytes 12000000 | tf_op jit(solution)/shard_map/near_field/pallas_call | solution.py:297
  67.5 0.4 all-to-all-done.1.got_ref
  67.9 8.6 %backward.1 = f32[2,128,256]{2,1,0:T(8,128)} custom-call(f32[32,16,128]{2,1,0:T(8,128)S(1)} %all-to-all-done.1.got_ref, f32[1536,1024]{1,0:T(8,128)} %interp_ref.3, f32[2,1024,256]{2,1,0:T(8,128)S(1)} %copy-done.4, f32[8,1536]{1,0:T(8,128)S(1)} %get-tuple-element.30.cos_ref, f32[8,1536]{1,0:T(8,128)S(1)} %get-tuple-element.29.sin_ref, ...), custom_call_target="tpu_custom_call" | custom-call | flops 3000000000 | bytes 9000000 | tf_op jit(solution)/shard_map/backward/pallas_call | solution.py:232
  (17 shorter events, 0.1 us)
Async XLA Ops:
  6.5 25.2 %copy-start = (f32[2,316,192]{1,2,0:T(8,128)S(1)}, f32[2,316,192]{1,2,0:T(8,128)}, u32[]{:S(2)}) copy-start(f32[2,316,192]{1,2,0:T(8,128)} %param.23) | copy-start | bytes 1456132
  6.5 52.1 %all-gather.3.cloned.1.call-start = ((), (), s32[]{:S(2)}) async-start(), calls=%async_computation.2 | async-start | bytes 1310720 | tf_op jit(solution)/shard_map/all_gather | solution.py:333
  6.5 6.7 %collective-permute-start = (bf16[2,128,256]{2,1,0:T(8,128)(2,1)}, bf16[2,128,256]{2,1,0:T(8,128)(2,1)S(1)}, u32[]{:S(2)}, u32[]{:S(2)}) collective-permute-start(bf16[2,128,256]{2,1,0:T(8,128)(2,1)} %cur_ref.1), channel_id=1, source_target_pairs={{0,1},{1,0},{2,3},{3,2},{4,5},{5,4},{6,7},{7,6},{8,9},{9,8},{10,11... | collective-permute-start | bytes 393224 | tf_op jit(solution)/shard_map/ppermute | solution.py:330
  14.9 0.9 %copy-start.2 = (bf16[2,128,256]{2,1,0:T(8,128)(2,1)S(1)}, bf16[2,128,256]{2,1,0:T(8,128)(2,1)}, u32[]{:S(2)}) copy-start(bf16[2,128,256]{2,1,0:T(8,128)(2,1)} %cur_ref.1) | copy-start | bytes 393220
  15.8 1.6 %copy-start.3 = (f32[2,1024,256]{2,1,0:T(8,128)S(1)}, f32[2,1024,256]{2,1,0:T(8,128)}, u32[]{:S(2)}) copy-start(f32[2,1024,256]{2,1,0:T(8,128)} %rad_ref.1) | copy-start | bytes 6291460
  25.6 24.2 %all-to-all-start = ((f32[32,16,128]{2,1,0:T(8,128)}), f32[32,16,128]{2,1,0:T(8,128)S(1)}, u32[]{:S(2)}, u32[]{:S(2)}) async-start(f32[32,16,128]{2,1,0:T(8,128)} %forward.1), calls=%async_computation | async-start | bytes 524288 | tf_op jit(solution)/shard_map/all_to_all | solution.py:342
  49.8 7.5 %copy-start.5 = (s32[40]{0:T(128)S(1)}, s32[40]{0:T(128)}, u32[]{:S(2)}) copy-start(s32[40]{0:T(128)} %param.18) | copy-start | bytes 484
  49.8 8.2 %copy-start.6 = (s32[40]{0:T(128)S(1)}, s32[40]{0:T(128)}, u32[]{:S(2)}) copy-start(s32[40]{0:T(128)} %param.17) | copy-start | bytes 484
  49.8 18.1 %copy-start.4 = (f32[2,1024,256]{2,1,0:T(8,128)S(1)}, f32[2,1024,256]{2,1,0:T(8,128)}, u32[]{:S(2)}) copy-start(f32[2,1024,256]{2,1,0:T(8,128)} %rec_ref.1) | copy-start | bytes 6291460
  54.7 13.2 %all-to-all-start.1 = ((f32[32,16,128]{2,1,0:T(8,128)}), f32[32,16,128]{2,1,0:T(8,128)S(1)}, u32[]{:S(2)}, u32[]{:S(2)}) async-start(f32[32,16,128]{2,1,0:T(8,128)} %bitcast.3), calls=%async_computation.1 | async-start | bytes 524288 | tf_op jit(solution)/shard_map/all_to_all | solution.py:350
  58.7 1.2 %copy-start.1 = (bf16[8,256,256]{2,1,0:T(8,128)(2,1)S(1)}, bf16[8,256,256]{2,1,0:T(8,128)(2,1)}, u32[]{:S(2)}) copy-start(bf16[8,256,256]{2,1,0:T(8,128)(2,1)} %all-gather.3.cloned.1.call-done) | copy-start | bytes 3145732
Sparse Core Ops, SparseCore 0:
  15.0 35.6 all-gather.2

commit v2 on v1

v2 whole, which is shorter than its diff:
```python
import functools
import jax
import jax.numpy as jnp
from jax import lax
from jax.experimental import pallas as pl
from jax.experimental.pallas import tpu as pltpu
from jax.sharding import PartitionSpec as P

F32 = jnp.float32
BF16 = jnp.bfloat16
VMEM_LIMIT = 24 << 20
HBM = pl.BlockSpec(memory_space=pltpu.HBM)
VMEM = pl.BlockSpec(memory_space=pltpu.VMEM)
SMEM = pl.BlockSpec(memory_space=pltpu.SMEM)
TILE = 512


def halves(x):
    high = x.astype(BF16)
    return high, (x - high.astype(F32)).astype(BF16)


def dot_nt(a, b):
    return lax.dot_general(a, b, (((1,), (1,)), ((), ())), preferred_element_type=F32)


def dot_nn(a, b):
    return lax.dot_general(a, b, (((1,), (0,)), ((), ())), preferred_element_type=F32)


def in_hbm(x):
    return pltpu.with_memory_space_constraint(x, pltpu.HBM)


def iota(shape, dim):
    return lax.broadcasted_iota(jnp.int32, shape, dim)


class Layout:
    def __init__(self, n_grp, n_ang, k_up, list_len):
        self.n_grp, self.n_ang = n_grp, n_ang
        self.n_dev = n_grp * n_ang
        self.own = k_up // self.n_dev
        self.pad = -(-self.own // 8) * 8
        self.list_len = list_len

    def first(self, dest):
        grp, ang = divmod(dest, self.n_ang)
        return (ang * self.n_grp + grp) * self.own


HALF = 64
NOTES = 48
CODE_BITS = 20
BIAS = 2048


def exponent(largest):
    return jnp.ceil(8.0 * jnp.log2(jnp.maximum(largest, 1e-30)))


def scale_of(eighths):
    return jnp.exp2(eighths * 0.125)


def pack(re, im, scale):
    def grid(x):
        return jnp.clip(jnp.round(x * (32767.0 / scale)), -32767.0, 32767.0).astype(jnp.int32)
    return jnp.bitwise_or(jnp.left_shift(grid(re), 16), jnp.bitwise_and(grid(im), 65535))


def unpack(words, scale):
    step = scale * (1.0 / 32767.0)
    re = jnp.right_shift(words, 16).astype(F32) * step
    im = jnp.right_shift(jnp.left_shift(words, 16), 16).astype(F32) * step
    return re, im


def note(word):
    return lax.shift_right_logical(word, CODE_BITS)


def fetch(source, target, sems, dim):
    def piece(i):
        at = (slice(None),) * dim + (pl.ds(pl.multiple_of(i * TILE, TILE), TILE),)
        return pltpu.make_async_copy(source.at[at], target.at[at], sems.at[i])

    for i in range(source.shape[dim] // TILE):
        piece(i).start()
    return lambda i: piece(i).wait()


def forward_kernel(lay, ang_ref, cur_hbm, phase_hbm, src_hbm, kind_hbm, cols_hbm, rad_hbm, interp_hbm, out_ref, cos_ref,
                   sin_ref, cur_ref, phase_ref, src_ref, kind_ref, cols_ref, rad_ref, interp_ref, high_ref, low_ref,
                   par_ref, code_ref, small_sems, rad_sems, interp_sems):
    small = [
        pltpu.make_async_copy(source, target, small_sems.at[i])
        for i, (source, target) in enumerate([
            (cur_hbm, cur_ref), (phase_hbm, phase_ref), (src_hbm, src_ref), (kind_hbm, kind_ref),
            (cols_hbm, cols_ref)])
    ]
    for copy in small:
        copy.start()
    rad_wait = fetch(rad_hbm, rad_ref, rad_sems, 1)
    interp_wait = fetch(interp_hbm, interp_ref, interp_sems, 0)
    for copy in small:
        copy.wait()
    count = cur_ref.shape[1]
    n_par = count // 8
    k_up, k_leaf = interp_ref.shape

    row = iota((count, count), 0)
    col = iota((count, count), 1)
    order = (col == (row % n_par) * 8 + row // n_par).astype(BF16)
    cur_re = dot_nn(order, cur_ref[0]).astype(BF16)
    cur_im = dot_nn(order, cur_ref[1]).astype(BF16)
    left = jnp.concatenate([cur_re, cur_im], axis=0)
    right = jnp.concatenate([-cur_im, cur_re], axis=0)
    cos_ref[...] = jnp.cos(phase_ref[...])
    sin_ref[...] = jnp.sin(phase_ref[...])

    src = src_ref[...]
    place = (jnp.left_shift(jnp.right_shift(src, 4), 3) + jnp.bitwise_and(src, 7)
             + jnp.bitwise_and(jnp.right_shift(src, 3), 1) * (lay.n_dev * n_par // 2))
    code_ref[:, 0:lay.list_len] = (place * 512 + kind_ref[...]).T
    codes = code_ref[pl.ds(pl.multiple_of(ang_ref[0] * n_par, n_par), n_par), 0:lay.list_len]
    n_ask = cols_ref.shape[1]
    asks = jnp.concatenate([cols_ref[...], jnp.zeros((1, 128 - n_ask), jnp.int32)], axis=1)
    asks = jnp.broadcast_to(asks, (8, 128)).T[:, 0:1]
    asks = [asks[b:b + n_par] for b in range(0, n_ask, n_par)]

    for i in range(k_leaf // TILE):
        rad_wait(i)
        at = pl.ds(i * TILE, TILE)
        rr_high, rr_low = halves(rad_ref[0, at, :])
        ri_high, ri_low = halves(rad_ref[1, at, :])
        radiated = (dot_nt(left, rr_high) + dot_nt(left, rr_low)
                    + dot_nt(right, ri_high) + dot_nt(right, ri_low))
        high, low = halves(radiated)
        high_ref[:, at] = high
        low_ref[:, at] = low

    for i in range(k_up // TILE):
        interp_wait(i)
        at = pl.ds(i * TILE, TILE)
        in_high, in_low = halves(interp_ref[at, :])
        children = (dot_nt(high_ref[...], in_high) + dot_nt(high_ref[...], in_low)
                    + dot_nt(low_ref[...], in_high))
        re_sum = im_sum = None
        for t in range(8):
            c = cos_ref[t:t + 1, at]
            s = sin_ref[t:t + 1, at]
            re = children[t * n_par:(t + 1) * n_par]
            im = children[count + t * n_par:count + (t + 1) * n_par]
            re_t = c * re - s * im
            im_t = c * im + s * re
            re_sum = re_t if t == 0 else re_sum + re_t
            im_sum = im_t if t == 0 else im_sum + im_t
        par_ref[0, :, at] = re_sum
        par_ref[1, :, at] = im_sum

    largest = jnp.max(jnp.maximum(jnp.abs(par_ref[0]), jnp.abs(par_ref[1])), axis=1, keepdims=True)
    eighths = exponent(largest)
    words = pack(par_ref[0], par_ref[1], scale_of(eighths))
    notes = [eighths.astype(jnp.int32) + BIAS] + asks
    notes.append(jnp.zeros((n_par, lay.list_len - len(notes)), jnp.int32))
    notes = codes + jnp.left_shift(jnp.concatenate(notes, axis=1), CODE_BITS)
    gap = [jnp.zeros((8, NOTES - lay.own), jnp.int32)] if lay.own < NOTES else []
    for dest in range(lay.n_dev):
        at = slice(lay.first(dest), lay.first(dest) + lay.own)
        out_ref[dest] = jnp.concatenate(
            [words[0:8, at], *gap, notes[0:8], words[8:16, at], *gap, notes[8:16]], axis=1)


def forward(lay, ang, current, radiate, interp, phase, sources, types, cols):
    count = current.shape[1]
    k_up, k_leaf = interp.shape
    n_par = count // 8
    return pl.pallas_call(
        functools.partial(forward_kernel, lay),
        in_specs=[SMEM] + [HBM] * 7,
        out_specs=[VMEM] * 3,
        out_shape=[
            jax.ShapeDtypeStruct((lay.n_dev, 8, 128), jnp.int32),
            jax.ShapeDtypeStruct(phase.shape, F32),
            jax.ShapeDtypeStruct(phase.shape, F32),
        ],
        scratch_shapes=[
            pltpu.VMEM(current.shape, BF16),
            pltpu.VMEM(phase.shape, F32),
            pltpu.VMEM(sources.shape[::-1], jnp.int32),
            pltpu.VMEM(types.shape[::-1], jnp.int32),
            pltpu.VMEM(cols.shape, jnp.int32),
            pltpu.VMEM(radiate.shape, F32),
            pltpu.VMEM(interp.shape, F32),
            pltpu.VMEM((2 * count, k_leaf), BF16),
            pltpu.VMEM((2 * count, k_leaf), BF16),
            pltpu.VMEM((2, n_par, k_up), F32),
            pltpu.VMEM((sources.shape[0], 128), jnp.int32),
            pltpu.SemaphoreType.DMA((5,)),
            pltpu.SemaphoreType.DMA((k_leaf // TILE,)),
            pltpu.SemaphoreType.DMA((k_up // TILE,)),
        ],
        compiler_params=pltpu.CompilerParams(vmem_limit_bytes=VMEM_LIMIT),
        cost_estimate=pl.CostEstimate(flops=3 * 10**9, bytes_accessed=9 * 10**6, transcendentals=0),
        name="forward",
    )(ang, *map(in_hbm, (current, phase, sources.T, types.T, cols, radiate, interp)))


def translate_kernel(lay, got_ref, table_ref, out_ref, x_ref, t_ref, acc_ref):
    n_par = 2 * got_ref.shape[0]
    side = n_par // 2
    span = 2 * lay.pad
    n_pad = table_ref.shape[1]
    got = got_ref[...].T
    codes = []
    for h in range(2):
        words = got[HALF * h:HALF * h + lay.pad]
        codes.append(got[HALF * h + NOTES:HALF * h + NOTES + lay.list_len])
        scale = scale_of((note(codes[h][0:1]) - BIAS).astype(F32))
        for part, value in enumerate(unpack(words, scale)):
            high, low = halves(value)
            at = lay.pad * part
            x_ref[at:at + lay.pad, side * h:side * h + side] = high
            x_ref[span + at:span + at + lay.pad, side * h:side * h + side] = low
    codes = jnp.bitwise_and(jnp.concatenate(codes, axis=1), (1 << CODE_BITS) - 1)
    high, low = halves(table_ref[...])
    t_ref[0:span] = high
    t_ref[span:2 * span] = low
    width = min(512, n_par)
    rows_src = iota((n_par, width), 0)
    rows_kind = iota((n_pad, width), 0)
    for p in range(0, n_par, width):
        at = slice(p, p + width)
        re_sum = im_sum = 0.0
        for m in range(lay.list_len):
            code = codes[m:m + 1, at]
            source = jnp.right_shift(code, 9)
            kind = jnp.bitwise_and(code, 511)
            pick = (rows_src == source).astype(BF16)
            both = dot_nn(x_ref[...], pick)
            chosen = both[0:span] + both[span:2 * span]
            pick = (rows_kind == kind).astype(BF16)
            both = dot_nn(t_ref[...], pick)
            factor = both[0:span] + both[span:2 * span]
            fr, fi = factor[0:lay.pad], factor[lay.pad:span]
            cr, ci = chosen[0:lay.pad], chosen[lay.pad:span]
            re_sum = re_sum + (fr * cr - fi * ci)
            im_sum = im_sum + (fr * ci + fi * cr)
        largest = jnp.maximum(jnp.max(jnp.abs(re_sum), axis=0, keepdims=True),
                              jnp.max(jnp.abs(im_sum), axis=0, keepdims=True))
        eighths = exponent(largest)
        acc_ref[0:lay.pad, at] = pack(re_sum, im_sum, scale_of(eighths))
        acc_ref[NOTES:NOTES + 8, at] = jnp.broadcast_to(eighths, (8, width)).astype(jnp.int32)
    for h in range(2):
        out_ref[:, HALF * h:HALF * h + HALF] = acc_ref[:, side * h:side * h + side].T


def translate_far(lay, got, table):
    n_par = 2 * got.shape[0]
    span = 2 * lay.pad
    return pl.pallas_call(
        functools.partial(translate_kernel, lay),
        in_specs=[VMEM] * 2,
        out_specs=VMEM,
        out_shape=jax.ShapeDtypeStruct(got.shape, jnp.int32),
        scratch_shapes=[
            pltpu.VMEM((2 * span, n_par), BF16),
            pltpu.VMEM((2 * span, table.shape[1]), BF16),
            pltpu.VMEM((HALF, n_par), jnp.int32),
        ],
        compiler_params=pltpu.CompilerParams(vmem_limit_bytes=VMEM_LIMIT),
        cost_estimate=pl.CostEstimate(flops=2 * 10**9, bytes_accessed=10**6, transcendentals=0),
        name="translate_far",
    )(got, table)


def backward_kernel(lay, got_ref, cos_ref, sin_ref, near_ref, interp_hbm, rec_hbm, out_ref,
                    interp_ref, rec_ref, inc_ref, high_ref, low_ref, interp_sems, rec_sems):
    interp_wait = fetch(interp_hbm, interp_ref, interp_sems, 1)
    rec_wait = fetch(rec_hbm, rec_ref, rec_sems, 1)
    count = near_ref.shape[1]
    n_par = count // 8

    for dest in range(lay.n_dev):
        words = got_ref[dest]
        j = lay.first(dest)
        for h in range(2):
            eighths = words[:, HALF * h + NOTES:HALF * h + NOTES + 1].astype(F32)
            values = unpack(words[:, HALF * h:HALF * h + lay.own], scale_of(eighths))
            for part in range(2):
                inc_ref[part, 8 * h:8 * h + 8, j:j + lay.own] = values[part]
    c = cos_ref[...]
    s = sin_ref[...]
    for p in range(0, n_par, 2):
        res, ims = [], []
        for q in (p, p + 1):
            re = inc_ref[0, q:q + 1, :]
            im = inc_ref[1, q:q + 1, :]
            res.append(c * re + s * im)
            ims.append(c * im - s * re)
        high, low = halves(jnp.concatenate(res, axis=0))
        high_ref[8 * p:8 * p + 16] = high
        low_ref[8 * p:8 * p + 16] = low
        high, low = halves(jnp.concatenate(ims, axis=0))
        high_ref[count + 8 * p:count + 8 * p + 16] = high
        low_ref[count + 8 * p:count + 8 * p + 16] = low

    re_sum, im_sum = near_ref[0], near_ref[1]
    for i in range(interp_ref.shape[1] // TILE):
        interp_wait(i)
        at = slice(i * TILE, i * TILE + TILE)
        in_high, in_low = halves(interp_ref[:, at])
        leaf = dot_nn(high_ref[...], in_high) + dot_nn(high_ref[...], in_low) + dot_nn(low_ref[...], in_high)
        leaf_high, leaf_low = halves(leaf)
        rec_wait(i)
        by = []
        for part in range(2):
            rec_high, rec_low = halves(rec_ref[part, at, :])
            by.append(dot_nn(leaf_high, rec_high) + dot_nn(leaf_high, rec_low) + dot_nn(leaf_low, rec_high))
        re_sum = re_sum + (by[0][0:count] - by[1][count:2 * count])
        im_sum = im_sum + (by[1][0:count] + by[0][count:2 * count])
    out_ref[0] = re_sum
    out_ref[1] = im_sum


def backward(lay, got, interp, receive, cosine, sine, near):
    count = near.shape[1]
    n_par = count // 8
    k_up, k_leaf = interp.shape
    unk = receive.shape[2]
    return pl.pallas_call(
        functools.partial(backward_kernel, lay),
        in_specs=[VMEM] * 4 + [HBM] * 2,
        out_specs=VMEM,
        out_shape=jax.ShapeDtypeStruct((2, count, unk), F32),
        scratch_shapes=[
            pltpu.VMEM(interp.shape, F32),
            pltpu.VMEM(receive.shape, F32),
            pltpu.VMEM((2, n_par, k_up), F32),
            pltpu.VMEM((2 * count, k_up), BF16),
            pltpu.VMEM((2 * count, k_up), BF16),
            pltpu.SemaphoreType.DMA((k_leaf // TILE,)),
            pltpu.SemaphoreType.DMA((k_leaf // TILE,)),
        ],
        compiler_params=pltpu.CompilerParams(vmem_limit_bytes=VMEM_LIMIT),
        cost_estimate=pl.CostEstimate(flops=3 * 10**9, bytes_accessed=9 * 10**6, transcendentals=0),
        name="backward",
    )(got, cosine, sine, near, in_hbm(interp), in_hbm(receive))


def pick_kernel(lay, n_block, me_ref, got_ref, cur_ref, *out_refs):
    count = cur_ref.shape[1]
    first = me_ref[0]
    ang = me_ref[1]
    for mask, out_ref in enumerate(out_refs):
        dest = first + jnp.bitwise_xor(ang, mask)
        notes = note(got_ref[dest])
        marks = []
        for field in range(1, 1 + -(-n_block // 16)):
            for h in range(2):
                lane = HALF * h + NOTES + field
                marks.append((iota((8, count), 1) == notes[:, lane:lane + 1] - ang * count).astype(F32))
        mark = jnp.concatenate(marks, axis=0).astype(BF16)
        for part in range(2):
            out_ref[part] = dot_nn(mark, cur_ref[part]).astype(BF16)


def pick_columns(lay, n_block, me, got, current):
    unk = current.shape[2]
    rows = -(-n_block // 16) * 16
    one = jax.ShapeDtypeStruct((2, rows, unk), BF16)
    return pl.pallas_call(
        functools.partial(pick_kernel, lay, n_block),
        in_specs=[SMEM, VMEM, VMEM],
        out_specs=[VMEM] * lay.n_ang,
        out_shape=[one] * lay.n_ang,
        compiler_params=pltpu.CompilerParams(vmem_limit_bytes=VMEM_LIMIT),
        cost_estimate=pl.CostEstimate(flops=10**8, bytes_accessed=10**6, transcendentals=0),
        name="pick_columns",
    )(me, got, current)


def swap(picked, n_ang):
    half = [picked[mask] for mask in range(0, n_ang, 2)]
    sent = jnp.stack([picked[mask] for mask in range(1, n_ang, 2)])
    got = lax.ppermute(sent, "ang", [(i, i ^ 1) for i in range(n_ang)])
    return [one + got[k] for k, one in enumerate(half)]


def answers(half, n_ang):
    return [half[0]] + [
        lax.ppermute(half[k], "ang", [(i, i ^ (2 * k)) for i in range(n_ang)]) for k in range(1, len(half))
    ]


def near_kernel(n_term, *refs):
    rows_ref, terms, (blocks_hbm, out_ref, blocks_ref, wide_ref, own_ref, sems) = (
        refs[0], refs[1:1 + n_term], refs[1 + n_term:])
    n_block, _, unk, _ = blocks_ref.shape
    here = n_block // sems.shape[0]

    def piece(i):
        at = pl.ds(i * here, here)
        return pltpu.make_async_copy(blocks_hbm.at[at], blocks_ref.at[at], sems.at[i])

    for i in range(sems.shape[0]):
        piece(i).start()
    wide_ref[...] = jnp.zeros_like(wide_ref)
    for part in range(2):
        total = terms[0][part].astype(F32)
        for term in terms[1:]:
            total = total + term[part].astype(F32)
        wide_ref[64 * part:64 * part + total.shape[0]] = total.astype(BF16)
    lane = iota((2 * unk, 128), 1) % 64
    own = jnp.zeros((2 * unk, 128), F32)
    for i in range(0, n_block, here):
        piece(i // here).wait()
        rows = blocks_ref[i:i + here].reshape(here * 2 * unk, unk)
        products = dot_nt(rows, wide_ref[...])
        for k in range(here):
            own = jnp.where(lane == i + k, products[2 * unk * k:2 * unk * (k + 1)], own)
    own_ref[...] = own

    by_block = own_ref[...].T
    by_re, by_im = by_block[:, 0:unk], by_block[:, unk:2 * unk]
    re = by_re[0:n_block] - by_im[64:64 + n_block]
    im = by_re[64:64 + n_block] + by_im[0:n_block]
    count = out_ref.shape[1]
    mark = (iota((count, n_block), 0) == rows_ref[...]).astype(BF16)
    for part, value in ((0, re), (1, im)):
        high, low = halves(value)
        out_ref[part] = dot_nn(mark, high) + dot_nn(mark, low)


def near_field(rows, terms, blocks, count):
    n_block, _, unk, _ = blocks.shape
    here = 4
    return pl.pallas_call(
        functools.partial(near_kernel, len(terms)),
        in_specs=[VMEM] * (1 + len(terms)) + [HBM],
        out_specs=VMEM,
        out_shape=jax.ShapeDtypeStruct((2, count, unk), F32),
        scratch_shapes=[
            pltpu.VMEM(blocks.shape, BF16),
            pltpu.VMEM((128, unk), BF16),
            pltpu.VMEM((2 * unk, 128), F32),
            pltpu.SemaphoreType.DMA((n_block // here,)),
        ],
        compiler_params=pltpu.CompilerParams(vmem_limit_bytes=VMEM_LIMIT),
        cost_estimate=pl.CostEstimate(flops=2 * 10**11, bytes_accessed=12 * 10**6, transcendentals=0),
        name="near_field",
    )(rows, *terms, in_hbm(blocks))


def on_device(n_grp, n_ang, current, near_blocks, near_rows, near_cols, radiate, receive, interp,
              shift_phase, translate, far_sources, far_types):
    count, unk = current.shape[1:]
    n_par = count // 8
    n_block = near_blocks.shape[0]
    k_up = interp.shape[0]
    n_kind = translate.shape[1]
    lay = Layout(n_grp, n_ang, k_up, far_sources.shape[1])
    grp = lax.axis_index("grp")
    ang = lax.axis_index("ang")
    axes = ("grp", "ang")

    message, cosine, sine = forward(
        lay, ang[None], current, radiate, interp, shift_phase, far_sources, far_types, near_cols[None])
    got = lax.all_to_all(message, axes, 0, 0)
    half = swap(pick_columns(lay, n_block, jnp.stack([grp * n_ang, ang]), got, current), n_ang)

    table = lax.dynamic_slice_in_dim(translate, grp * lay.own, lay.own, 2)
    kind_pad = -(-n_kind // 128) * 128
    table = jnp.pad(table, ((0, 0), (0, kind_pad - n_kind), (0, lay.pad - lay.own)))
    table = jnp.transpose(table, (0, 2, 1)).reshape(2 * lay.pad, kind_pad)

    incoming = translate_far(lay, got.reshape(lay.n_dev * 8, 128), table)
    incoming, half = lax.optimization_barrier((incoming, half))
    near = near_field(near_rows[None], answers(half, n_ang), near_blocks, count)
    returned = lax.all_to_all(incoming.reshape(lay.n_dev, 8, 128), axes, 0, 0)

    return backward(lay, returned, interp, receive, cosine, sine, near)


def solution(mesh):
    both = ("grp", "ang")
    in_specs = (
        P(None, both, None),
        P(both, None, None, None),
        P(both),
        P(both),
        P(),
        P(),
        P(),
        P(),
        P(None, None, "ang"),
        P("grp", None),
        P("grp", None),
    )
    run = functools.partial(on_device, mesh.shape["grp"], mesh.shape["ang"])
    return jax.shard_map(run, mesh=mesh, in_specs=in_specs, out_specs=P(None, both, None), check_vma=False)
```

time: 84 us -> 57.8 us (0.69)
  between operations: 13.5 us -> 0.28 us
  waiting for transfers between devices: 20.2 us -> 8.71 us
  local copies, waits for them, and re-layouts: 5.77 us -> 0.04 us
  starting transfers between devices: 11.6 us -> 16.5 us
  other arithmetic: 2.86 us -> 0.13 us
  Pallas kernels: 29.3 us -> 31.9 us
    all_to_all x1, waiting for transfers between devices: 18 us -> 7.66 us  [on_device(): got = lax.all_to_all(message, axes, 0, 0)]
    unnamed x16 -> x6, local copies, waits for them, and re-layouts: 3.86 us -> 0.01 us
    ppermute x1 -> x4, starting transfers between devices: 2.97 us -> 5.75 us  [the longest x3 4.45 us: answers(): lax.ppermute(half[k], 'ang', [(i, i ^ 2 * k) for i in range(n_ang)])]
    pallas_call x4 -> x5, Pallas kernels: 29.3 us -> 31.9 us  [the longest x1 9.88 us: backward(): pl.pallas_call(functools.partial(backward_kernel, lay), in_specs=[VMEM] *...]
    concatenate x1 -> x0, other arithmetic: 1.64 us -> none  [on_device(): pair = jnp.concatenate([current, swapped], axis=1)]
    all_to_all x1, starting transfers between devices: 6.09 us -> 7.31 us  [on_device(): got = lax.all_to_all(message, axes, 0, 0)]
    another operation x3 -> x2, other arithmetic: 1.22 us -> 0.1 us  [the longest x1 0.08 us: on_device(): jnp.stack([grp * n_ang, ang])]
    sin x1 -> x0, local copies, waits for them, and re-layouts: 0.98 us -> none  [on_device(): sine = jnp.sin(shift_phase)]
  transfers between devices with their start and end apart: 4 -> 6, of which waited for: 3 -> 2; matrix products, arithmetic and copies ran while one was open for 4% -> 0% of each run, Pallas kernels for 25% -> 23%
where the time goes in v2:
time: 57.8 us; the launch traced here: 57.5 us
  Pallas kernels  31.9 us (55%)
  starting transfers between devices  16.5 us (29%)
  waiting for transfers between devices  8.71 us (15%)
    pallas_call x1, Pallas kernels, backward(): pl.pallas_call(functools.partial(backward_kernel, lay), in_specs=[VMEM] *...  9.88 us
    pallas_call x1, Pallas kernels, near_field(): pl.pallas_call(functools.partial(near_kernel, len(terms)), in_specs=[VMEM...  8.52 us
    pallas_call x1, Pallas kernels, forward(): pl.pallas_call(functools.partial(forward_kernel, lay), in_specs=[SMEM] +...  7.97 us
    all_to_all x1, waiting for transfers between devices, on_device(): got = lax.all_to_all(message, axes, 0, 0)  7.66 us
    all_to_all x1, starting transfers between devices, on_device(): got = lax.all_to_all(message, axes, 0, 0)  7.31 us
    pallas_call x1, Pallas kernels, translate_far(): pl.pallas_call(functools.partial(translate_kernel, lay), in_specs=[VMEM]...  4.6 us
    ppermute x3, starting transfers between devices, answers(): lax.ppermute(half[k], 'ang', [(i, i ^ 2 * k) for i in range(n_ang)])  4.45 us
    all_to_all x1, starting transfers between devices, on_device(): returned = lax.all_to_all(incoming.reshape(lay.n_dev, 8, 128), axes, 0, 0)  3.47 us
  transfers between devices with their start and end apart: 6, of which 2 were waited for; matrix products, arithmetic and copies ran while one was open for 0% of the time, Pallas kernels for 23%

profile of v2, /device:TPU:0, one launch (start us, length us, event | category | flops | bytes accessed | tf_op | source)
XLA Modules:
  0.0 57.5 jit_solution(11611448119961591005)
XLA Ops:
  0.0 0.0 copy-start
  0.0 0.0 copy-start.1
  0.0 8.0 %forward.1 = (s32[32,8,128]{2,1,0:T(8,128)}, f32[8,1536]{1,0:T(8,128)S(1)}, f32[8,1536]{1,0:T(8,128)S(1)}) custom-call(s32[1]{0:T(128)} %bitcast.ang_ref, bf16[2,128,256]{2,1,0:T(8,128)(2,1)} %cur_ref.1, f32[8,1536]{1,0:T(8,128)} %phase_hbm.1, s32[16,128]{1,0:T(8,128)} %bitcast.38, s32[16,128]{1,0:T(8,128)} %bitcast.39, s32[1,40]{1,0:T(1,128)} %bitcast.40, ...), custom_call_target="tpu_custom_call" | custom-call | flops 3000000000 | bytes 9000000 | tf_op jit(solution)/shard_map/forward/pallas_call | solution.py:179
  8.0 0.0 copy-start.2
  8.0 7.3 %all-to-all-start = ((s32[32,8,128]{2,1,0:T(8,128)}), s32[32,8,128]{2,1,0:T(8,128)S(1)}, u32[]{:S(2)}, u32[]{:S(2)}) async-start(s32[32,8,128]{2,1,0:T(8,128)} %get-tuple-element.21), calls=%async_computation | async-start | bytes 262144 | tf_op jit(solution)/shard_map/all_to_all | solution.py:470
  15.3 0.1 pad_add_fusion.me_ref
  15.4 7.7 %all-to-all-done.got_ref = s32[32,8,128]{2,1,0:T(8,128)S(1)} async-done(((s32[32,8,128]{2,1,0:T(8,128)}), s32[32,8,128]{2,1,0:T(8,128)S(1)}, u32[]{:S(2)}, u32[]{:S(2)}) %all-to-all-start) | async-done | bytes 131104 | tf_op jit(solution)/shard_map/all_to_all | solution.py:470
  23.1 0.0 copy-done.1
  23.1 0.9 %pick_columns.1 = (bf16[2,48,256]{2,1,0:T(8,128)(2,1)S(1)}, bf16[2,48,256]{2,1,0:T(8,128)(2,1)S(1)}, bf16[2,48,256]{2,1,0:T(8,128)(2,1)S(1)}, bf16[2,48,256]{2,1...) custom-call(s32[2]{0:T(128)S(1)} %pad_add_fusion.me_ref, ...), custom_call_target="tpu_custom_call" | custom-call | flops 100000000 | bytes 1000000 | tf_op jit(solution)/shard_map/pick_columns/pallas_call | solution.py:373
  24.0 1.3 %collective-permute-start = (bf16[4,2,48,256]{3,2,1,0:T(8,128)(2,1)S(1)}, bf16[4,2,48,256]{3,2,1,0:T(8,128)(2,1)S(1)}, u32[]{:S(2)}, u32[]{:S(2)}) collective-permute-start(bf16[4,2,48,256]{3,2,1,0:T(8,128)(2,1)S(1)} %pad_maximum_fusion), channel_id=1, source_target_pairs={{0,1},{1,0},{2,3},{3,2},{4,5},{5,4},{6,7},{7,6},{8,9},{9,8},{10,11... | collective-permute-start | bytes 589832 | tf_op jit(solution)/shard_map/ppermute | solution.py:387
  25.3 0.0 copy-done
  25.3 4.6 %translate_far.1 = s32[256,128]{1,0:T(8,128)} custom-call(s32[256,128]{1,0:T(8,128)S(1)} %bitcast.32, f32[96,384]{1,0:T(8,128)S(1)} %bitcast.31), custom_call_target="tpu_custom_call" | custom-call | flops 2000000000 | bytes 1000000 | tf_op jit(solution)/shard_map/translate_far/pallas_call | solution.py:262
  29.9 1.0 %collective-permute-done = bf16[4,2,48,256]{3,2,1,0:T(8,128)(2,1)S(1)} collective-permute-done((bf16[4,2,48,256]{3,2,1,0:T(8,128)(2,1)S(1)}, bf16[4,2,48,256]{3,2,1,0:T(8,128)(2,1)S(1)}, u32[]{:S(2)}, u32[]{:S(2)}) %collective-permute-start) | collective-permute-done | bytes 196640 | tf_op jit(solution)/shard_map/ppermute | solution.py:387
  31.0 0.6 %collective-permute-start.1 = (bf16[2,48,256]{2,1,0:T(8,128)(2,1)S(1)}, bf16[2,48,256]{2,1,0:T(8,128)(2,1)S(1)}, u32[]{:S(2)}, u32[]{:S(2)}) collective-permute-start(bf16[2,48,256]{2,1,0:T(8,128)(2,1)S(1)} %get-tuple-element.34), channel_id=1, source_target_pairs={{0,2},{1,3},{2,0},{3,1},{4,6},{5,7},{6,4},{7,5},{8,10},{9,11},{10,... | collective-permute-start | bytes 147464 | tf_op jit(solution)/shard_map/ppermute | solution.py:393
  31.6 1.0 %collective-permute-start.2 = (bf16[2,48,256]{2,1,0:T(8,128)(2,1)S(1)}, bf16[2,48,256]{2,1,0:T(8,128)(2,1)S(1)}, u32[]{:S(2)}, u32[]{:S(2)}) collective-permute-start(bf16[2,48,256]{2,1,0:T(8,128)(2,1)S(1)} %get-tuple-element.35), channel_id=1, source_target_pairs={{0,4},{1,5},{2,6},{3,7},{4,0},{5,1},{6,2},{7,3},{8,12},{9,13},{10,... | collective-permute-start | bytes 147464 | tf_op jit(solution)/shard_map/ppermute | solution.py:393
  32.7 2.8 %collective-permute-start.3 = (bf16[2,48,256]{2,1,0:T(8,128)(2,1)S(1)}, bf16[2,48,256]{2,1,0:T(8,128)(2,1)S(1)}, u32[]{:S(2)}, u32[]{:S(2)}) collective-permute-start(bf16[2,48,256]{2,1,0:T(8,128)(2,1)S(1)} %get-tuple-element.36), channel_id=1, source_target_pairs={{0,6},{1,7},{2,4},{3,5},{4,2},{5,3},{6,0},{7,1},{8,14},{9,15},{10,... | collective-permute-start | bytes 147464 | tf_op jit(solution)/shard_map/ppermute | solution.py:393
  35.4 3.5 %all-to-all-start.1 = ((s32[32,8,128]{2,1,0:T(8,128)}), s32[32,8,128]{2,1,0:T(8,128)}, u32[]{:S(2)}, u32[]{:S(2)}) async-start(s32[32,8,128]{2,1,0:T(8,128)} %bitcast.16), calls=%async_computation.1 | async-start | bytes 262144 | tf_op jit(solution)/shard_map/all_to_all | solution.py:481
  38.9 0.0 collective-permute-done.1.refs_2_
  38.9 0.0 collective-permute-done.2.refs_3_
  38.9 0.0 collective-permute-done.3.refs_4_
  39.0 0.0 copy-done.2
  39.0 8.5 %near_field.1.near_ref = f32[2,128,256]{2,1,0:T(8,128)S(1)} custom-call(s32[1,40]{1,0:T(1,128)S(1)} %bitcast.37, bf16[2,48,256]{2,1,0:T(8,128)(2,1)S(1)} %get-tuple-element.33.refs_1_, bf16[2,48,256]{2,1,0:T(8,128)(2,1)S(1)} %collective-permute-done.1.refs_2_, bf16[2,48,256]{2,1,0:T(8,128)(2,1)S(1)} %collective-permute-done.2.refs_3_, ...), custom_call_target="tpu_custom_call" | custom-call | flops 199999995904 | bytes 12000000 | tf_op jit(solution)/shard_map/near_field/pallas_call | solution.py:439
  47.5 0.0 all-to-all-done.1.got_ref
  47.5 9.9 %backward.1 = f32[2,128,256]{2,1,0:T(8,128)} custom-call(s32[32,8,128]{2,1,0:T(8,128)} %all-to-all-done.1.got_ref, f32[8,1536]{1,0:T(8,128)S(1)} %get-tuple-element.31.cos_ref, f32[8,1536]{1,0:T(8,128)S(1)} %get-tuple-element.32.sin_ref, f32[2,128,256]{2,1,0:T(8,128)S(1)} %near_field.1.near_ref, f32[1536,1024]{1,0:T(8,128)} %interp_hbm.3, ...), custom_call_target="tpu_custom_call" | custom-call | flops 3000000000 | bytes 9000000 | tf_op jit(solution)/shard_map/backward/pallas_call | solution.py:332
  (4 shorter events, 0.1 us)
Async XLA Ops:
  0.0 25.3 %copy-start = (f32[2,316,192]{1,2,0:T(8,128)S(1)}, f32[2,316,192]{1,2,0:T(8,128)}, u32[]{:S(2)}) copy-start(f32[2,316,192]{1,2,0:T(8,128)} %param.19) | copy-start | bytes 1456132
  0.0 23.1 %copy-start.1 = (bf16[2,128,256]{2,1,0:T(8,128)(2,1)S(1)}, bf16[2,128,256]{2,1,0:T(8,128)(2,1)}, u32[]{:S(2)}) copy-start(bf16[2,128,256]{2,1,0:T(8,128)(2,1)} %cur_ref.1) | copy-start | bytes 393220
  8.0 31.0 %copy-start.2 = (s32[40]{0:T(128)S(1)}, s32[40]{0:T(128)}, u32[]{:S(2)}) copy-start(s32[40]{0:T(128)} %param.13) | copy-start | bytes 484
  8.0 15.1 %all-to-all-start = ((s32[32,8,128]{2,1,0:T(8,128)}), s32[32,8,128]{2,1,0:T(8,128)S(1)}, u32[]{:S(2)}, u32[]{:S(2)}) async-start(s32[32,8,128]{2,1,0:T(8,128)} %get-tuple-element.21), calls=%async_computation | async-start | bytes 262144 | tf_op jit(solution)/shard_map/all_to_all | solution.py:470
  24.0 7.0 %collective-permute-start = (bf16[4,2,48,256]{3,2,1,0:T(8,128)(2,1)S(1)}, bf16[4,2,48,256]{3,2,1,0:T(8,128)(2,1)S(1)}, u32[]{:S(2)}, u32[]{:S(2)}) collective-permute-start(bf16[4,2,48,256]{3,2,1,0:T(8,128)(2,1)S(1)} %pad_maximum_fusion), channel_id=1, source_target_pairs={{0,1},{1,0},{2,3},{3,2},{4,5},{5,4},{6,7},{7,6},{8,9},{9,8},{10,11... | collective-permute-start | bytes 589832 | tf_op jit(solution)/shard_map/ppermute | solution.py:387
  31.0 7.9 %collective-permute-start.1 = (bf16[2,48,256]{2,1,0:T(8,128)(2,1)S(1)}, bf16[2,48,256]{2,1,0:T(8,128)(2,1)S(1)}, u32[]{:S(2)}, u32[]{:S(2)}) collective-permute-start(bf16[2,48,256]{2,1,0:T(8,128)(2,1)S(1)} %get-tuple-element.34), channel_id=1, source_target_pairs={{0,2},{1,3},{2,0},{3,1},{4,6},{5,7},{6,4},{7,5},{8,10},{9,11},{10,... | collective-permute-start | bytes 147464 | tf_op jit(solution)/shard_map/ppermute | solution.py:393
  31.6 7.3 %collective-permute-start.2 = (bf16[2,48,256]{2,1,0:T(8,128)(2,1)S(1)}, bf16[2,48,256]{2,1,0:T(8,128)(2,1)S(1)}, u32[]{:S(2)}, u32[]{:S(2)}) collective-permute-start(bf16[2,48,256]{2,1,0:T(8,128)(2,1)S(1)} %get-tuple-element.35), channel_id=1, source_target_pairs={{0,4},{1,5},{2,6},{3,7},{4,0},{5,1},{6,2},{7,3},{8,12},{9,13},{10,... | collective-permute-start | bytes 147464 | tf_op jit(solution)/shard_map/ppermute | solution.py:393
  32.7 6.3 %collective-permute-start.3 = (bf16[2,48,256]{2,1,0:T(8,128)(2,1)S(1)}, bf16[2,48,256]{2,1,0:T(8,128)(2,1)S(1)}, u32[]{:S(2)}, u32[]{:S(2)}) collective-permute-start(bf16[2,48,256]{2,1,0:T(8,128)(2,1)S(1)} %get-tuple-element.36), channel_id=1, source_target_pairs={{0,6},{1,7},{2,4},{3,5},{4,2},{5,3},{6,0},{7,1},{8,14},{9,15},{10,... | collective-permute-start | bytes 147464 | tf_op jit(solution)/shard_map/ppermute | solution.py:393
  35.4 12.1 %all-to-all-start.1 = ((s32[32,8,128]{2,1,0:T(8,128)}), s32[32,8,128]{2,1,0:T(8,128)}, u32[]{:S(2)}, u32[]{:S(2)}) async-start(s32[32,8,128]{2,1,0:T(8,128)} %bitcast.16), calls=%async_computation.1 | async-start | bytes 262144 | tf_op jit(solution)/shard_map/all_to_all | solution.py:481

commit v3 on v2

--- a/solution.py
+++ b/solution.py
@@ -13,6 +13,7 @@
 VMEM = pl.BlockSpec(memory_space=pltpu.VMEM)
 SMEM = pl.BlockSpec(memory_space=pltpu.SMEM)
 TILE = 512
+ROWS = 512
 
 
 def halves(x):
@@ -80,14 +81,11 @@
     return lax.shift_right_logical(word, CODE_BITS)
 
 
-def fetch(source, target, sems, dim):
-    def piece(i):
-        at = (slice(None),) * dim + (pl.ds(pl.multiple_of(i * TILE, TILE), TILE),)
-        return pltpu.make_async_copy(source.at[at], target.at[at], sems.at[i])
-
-    for i in range(source.shape[dim] // TILE):
-        piece(i).start()
-    return lambda i: piece(i).wait()
+def piece(source, target, sems, dim, size):
+    def at(i):
+        index = (slice(None),) * dim + (pl.ds(pl.multiple_of(i * size, size), size),)
+        return pltpu.make_async_copy(source.at[index], target.at[index], sems.at[i])
+    return at
 
 
 def forward_kernel(lay, ang_ref, cur_hbm, phase_hbm, src_hbm, kind_hbm, cols_hbm, rad_hbm, interp_hbm, out_ref, cos_ref,
@@ -101,8 +99,12 @@
     ]
     for copy in small:
         copy.start()
-    rad_wait = fetch(rad_hbm, rad_ref, rad_sems, 1)
-    interp_wait = fetch(interp_hbm, interp_ref, interp_sems, 0)
+    rad_piece = piece(rad_hbm, rad_ref, rad_sems, 1, TILE)
+    interp_piece = piece(interp_hbm, interp_ref, interp_sems, 0, ROWS)
+    n_rad, n_interp = rad_sems.shape[0], interp_sems.shape[0]
+    for i in range(n_rad):
+        rad_piece(i).start()
+    interp_piece(0).start()
     for copy in small:
         copy.wait()
     count = cur_ref.shape[1]
@@ -129,9 +131,14 @@
     asks = jnp.broadcast_to(asks, (8, 128)).T[:, 0:1]
     asks = [asks[b:b + n_par] for b in range(0, n_ask, n_par)]
 
-    for i in range(k_leaf // TILE):
-        rad_wait(i)
-        at = pl.ds(i * TILE, TILE)
+    def radiate_tile(i, carry):
+        rad_piece(i).wait()
+
+        @pl.when(i + 1 < n_interp)
+        def _():
+            interp_piece(i + 1).start()
+
+        at = pl.ds(pl.multiple_of(i * TILE, TILE), TILE)
         rr_high, rr_low = halves(rad_ref[0, at, :])
         ri_high, ri_low = halves(rad_ref[1, at, :])
         radiated = (dot_nt(left, rr_high) + dot_nt(left, rr_low)
@@ -139,10 +146,18 @@
         high, low = halves(radiated)
         high_ref[:, at] = high
         low_ref[:, at] = low
-
-    for i in range(k_up // TILE):
-        interp_wait(i)
-        at = pl.ds(i * TILE, TILE)
+        return carry
+
+    lax.fori_loop(0, n_rad, radiate_tile, 0)
+
+    def interp_tile(i, carry):
+        interp_piece(i).wait()
+
+        @pl.when(i + 1 + n_rad < n_interp)
+        def _():
+            interp_piece(i + 1 + n_rad).start()
+
+        at = pl.ds(pl.multiple_of(i * ROWS, ROWS), ROWS)
         in_high, in_low = halves(interp_ref[at, :])
         children = (dot_nt(high_ref[...], in_high) + dot_nt(high_ref[...], in_low)
                     + dot_nt(low_ref[...], in_high))
@@ -158,6 +173,9 @@
             im_sum = im_t if t == 0 else im_sum + im_t
         par_ref[0, :, at] = re_sum
         par_ref[1, :, at] = im_sum
+        return carry
+
+    lax.fori_loop(0, n_interp, interp_tile, 0)
 
     largest = jnp.max(jnp.maximum(jnp.abs(par_ref[0]), jnp.abs(par_ref[1])), axis=1, keepdims=True)
     eighths = exponent(largest)
@@ -199,7 +217,7 @@
             pltpu.VMEM((sources.shape[0], 128), jnp.int32),
             pltpu.SemaphoreType.DMA((5,)),
             pltpu.SemaphoreType.DMA((k_leaf // TILE,)),
-            pltpu.SemaphoreType.DMA((k_up // TILE,)),
+            pltpu.SemaphoreType.DMA((k_up // ROWS,)),
         ],
         compiler_params=pltpu.CompilerParams(vmem_limit_bytes=VMEM_LIMIT),
         cost_estimate=pl.CostEstimate(flops=3 * 10**9, bytes_accessed=9 * 10**6, transcendentals=0),
@@ -276,9 +294,12 @@
 
 
 def backward_kernel(lay, got_ref, cos_ref, sin_ref, near_ref, interp_hbm, rec_hbm, out_ref,
-                    interp_ref, rec_ref, inc_ref, high_ref, low_ref, interp_sems, rec_sems):
-    interp_wait = fetch(interp_hbm, interp_ref, interp_sems, 1)
-    rec_wait = fetch(rec_hbm, rec_ref, rec_sems, 1)
+                    interp_ref, rec_ref, inc_ref, high_ref, low_ref, leaf_ref, interp_sems, rec_sems):
+    interp_piece = piece(interp_hbm, interp_ref, interp_sems, 0, ROWS)
+    rec_piece = piece(rec_hbm, rec_ref, rec_sems, 1, TILE)
+    n_interp, n_rec = interp_sems.shape[0], rec_sems.shape[0]
+    for i in range(3):
+        interp_piece(i).start()
     count = near_ref.shape[1]
     n_par = count // 8
 
@@ -306,20 +327,37 @@
         high_ref[count + 8 * p:count + 8 * p + 16] = high
         low_ref[count + 8 * p:count + 8 * p + 16] = low
 
-    re_sum, im_sum = near_ref[0], near_ref[1]
-    for i in range(interp_ref.shape[1] // TILE):
-        interp_wait(i)
-        at = slice(i * TILE, i * TILE + TILE)
-        in_high, in_low = halves(interp_ref[:, at])
-        leaf = dot_nn(high_ref[...], in_high) + dot_nn(high_ref[...], in_low) + dot_nn(low_ref[...], in_high)
-        leaf_high, leaf_low = halves(leaf)
-        rec_wait(i)
-        by = []
-        for part in range(2):
-            rec_high, rec_low = halves(rec_ref[part, at, :])
-            by.append(dot_nn(leaf_high, rec_high) + dot_nn(leaf_high, rec_low) + dot_nn(leaf_low, rec_high))
-        re_sum = re_sum + (by[0][0:count] - by[1][count:2 * count])
-        im_sum = im_sum + (by[1][0:count] + by[0][count:2 * count])
+    leaf_ref[...] = jnp.zeros_like(leaf_ref)
+
+    def leaf_tile(i, carry):
+        interp_piece(i).wait()
+
+        @pl.when(i + 3 < n_interp)
+        def _():
+            interp_piece(i + 3).start()
+
+        @pl.when(i + 3 >= n_interp)
+        def _():
+            @pl.when(i + 3 - n_interp < n_rec)
+            def _():
+                rec_piece(i + 3 - n_interp).start()
+
+        at = pl.ds(pl.multiple_of(i * ROWS, ROWS), ROWS)
+        in_high, in_low = halves(interp_ref[at, :])
+        leaf_ref[...] += (dot_nn(high_ref[:, at], in_high) + dot_nn(high_ref[:, at], in_low)
+                          + dot_nn(low_ref[:, at], in_high))
+        return carry
+
+    lax.fori_loop(0, n_interp, leaf_tile, 0)
+    for i in range(n_rec):
+        rec_piece(i).wait()
+    leaf_high, leaf_low = halves(leaf_ref[...])
+    by = []
+    for part in range(2):
+        rec_high, rec_low = halves(rec_ref[part])
+        by.append(dot_nn(leaf_high, rec_high) + dot_nn(leaf_high, rec_low) + dot_nn(leaf_low, rec_high))
+    re_sum = near_ref[0] + (by[0][0:count] - by[1][count:2 * count])
+    im_sum = near_ref[1] + (by[1][0:count] + by[0][count:2 * count])
     out_ref[0] = re_sum
     out_ref[1] = im_sum
 
@@ -340,13 +378,14 @@
             pltpu.VMEM((2, n_par, k_up), F32),
             pltpu.VMEM((2 * count, k_up), BF16),
             pltpu.VMEM((2 * count, k_up), BF16),
-            pltpu.SemaphoreType.DMA((k_leaf // TILE,)),
+            pltpu.VMEM((2 * count, k_leaf), F32),
+            pltpu.SemaphoreType.DMA((k_up // ROWS,)),
             pltpu.SemaphoreType.DMA((k_leaf // TILE,)),
         ],
         compiler_params=pltpu.CompilerParams(vmem_limit_bytes=VMEM_LIMIT),
         cost_estimate=pl.CostEstimate(flops=3 * 10**9, bytes_accessed=9 * 10**6, transcendentals=0),
         name="backward",
-    )(got, cosine, sine, near, in_hbm(interp), in_hbm(receive))
+    )(pltpu.with_memory_space_constraint(got, pltpu.VMEM), cosine, sine, near, in_hbm(interp), in_hbm(receive))
 
 
 def pick_kernel(lay, n_block, me_ref, got_ref, cur_ref, *out_refs):
@@ -362,14 +401,13 @@
                 lane = HALF * h + NOTES + field
                 marks.append((iota((8, count), 1) == notes[:, lane:lane + 1] - ang * count).astype(F32))
         mark = jnp.concatenate(marks, axis=0).astype(BF16)
-        for part in range(2):
-            out_ref[part] = dot_nn(mark, cur_ref[part]).astype(BF16)
+        both = [dot_nn(mark, cur_ref[part])[0:n_block] for part in range(2)]
+        out_ref[...] = jnp.concatenate(both, axis=0).astype(BF16)
 
 
 def pick_columns(lay, n_block, me, got, current):
     unk = current.shape[2]
-    rows = -(-n_block // 16) * 16
-    one = jax.ShapeDtypeStruct((2, rows, unk), BF16)
+    one = jax.ShapeDtypeStruct((2 * n_block, unk), BF16)
     return pl.pallas_call(
         functools.partial(pick_kernel, lay, n_block),
         in_specs=[SMEM, VMEM, VMEM],
@@ -400,27 +438,34 @@
     n_block, _, unk, _ = blocks_ref.shape
     here = n_block // sems.shape[0]
 
-    def piece(i):
-        at = pl.ds(i * here, here)
-        return pltpu.make_async_copy(blocks_hbm.at[at], blocks_ref.at[at], sems.at[i])
-
-    for i in range(sems.shape[0]):
-        piece(i).start()
-    wide_ref[...] = jnp.zeros_like(wide_ref)
-    for part in range(2):
-        total = terms[0][part].astype(F32)
-        for term in terms[1:]:
-            total = total + term[part].astype(F32)
-        wide_ref[64 * part:64 * part + total.shape[0]] = total.astype(BF16)
+    block_piece = piece(blocks_hbm, blocks_ref, sems, 0, here)
+    n_piece = sems.shape[0]
+    for i in range(3):
+        block_piece(i).start()
+    total = terms[0][...].astype(F32)
+    for term in terms[1:]:
+        total = total + term[...].astype(F32)
+    gap = jnp.zeros((64 - n_block, unk), F32)
+    wide_ref[...] = jnp.concatenate([total[0:n_block], gap, total[n_block:], gap], axis=0).astype(BF16)
     lane = iota((2 * unk, 128), 1) % 64
-    own = jnp.zeros((2 * unk, 128), F32)
-    for i in range(0, n_block, here):
-        piece(i // here).wait()
-        rows = blocks_ref[i:i + here].reshape(here * 2 * unk, unk)
+    own_ref[...] = jnp.zeros_like(own_ref)
+
+    def some_blocks(i, carry):
+        block_piece(i).wait()
+
+        @pl.when(i + 3 < n_piece)
+        def _():
+            block_piece(i + 3).start()
+
+        rows = blocks_ref[pl.ds(i * here, here)].reshape(here * 2 * unk, unk)
         products = dot_nt(rows, wide_ref[...])
+        own = own_ref[...]
         for k in range(here):
-            own = jnp.where(lane == i + k, products[2 * unk * k:2 * unk * (k + 1)], own)
-    own_ref[...] = own
+            own = jnp.where(lane == i * here + k, products[2 * unk * k:2 * unk * (k + 1)], own)
+        own_ref[...] = own
+        return carry
+
+    lax.fori_loop(0, n_piece, some_blocks, 0)
 
     by_block = own_ref[...].T
     by_re, by_im = by_block[:, 0:unk], by_block[:, unk:2 * unk]
@@ -435,7 +480,7 @@
 
 def near_field(rows, terms, blocks, count):
     n_block, _, unk, _ = blocks.shape
-    here = 4
+    here = 8
     return pl.pallas_call(
         functools.partial(near_kernel, len(terms)),
         in_specs=[VMEM] * (1 + len(terms)) + [HBM],

time: 57.8 us -> 52.1 us (0.901)
  Pallas kernels: 31.9 us -> 25.1 us
  waiting for transfers between devices: 8.71 us -> 10.1 us
    pallas_call x1, Pallas kernels: 8.52 us -> 5.52 us  [near_field(): pl.pallas_call(functools.partial(near_kernel, len(terms)), in_specs=[VMEM...]
    pallas_call x1, Pallas kernels: 9.88 us -> 7.35 us  [backward(): pl.pallas_call(functools.partial(backward_kernel, lay), in_specs=[VMEM] *...]
    all_to_all x1, waiting for transfers between devices: 0.01 us -> 2.15 us  [on_device(): returned = lax.all_to_all(incoming.reshape(lay.n_dev, 8, 128), axes, 0, 0)]
    pallas_call x1, Pallas kernels: 7.97 us -> 6.75 us  [forward(): pl.pallas_call(functools.partial(forward_kernel, lay), in_specs=[SMEM] +...]
    ppermute x1, waiting for transfers between devices: 1.05 us -> 0.39 us  [swap(): got = lax.ppermute(sent, 'ang', [(i, i ^ 1) for i in range(n_ang)])]
  transfers between devices with their start and end apart: 6 -> 6, of which waited for: 2 -> 3; matrix products, arithmetic and copies ran while one was open for 0% -> 0% of each run, Pallas kernels for 23% -> 19%
where the time goes in v3:
time: 52.1 us; the launch traced here: 51.9 us
  Pallas kernels  25.1 us (48%)
  starting transfers between devices  16.3 us (31%)
  waiting for transfers between devices  10.1 us (19%)
    all_to_all x1, waiting for transfers between devices, on_device(): got = lax.all_to_all(message, axes, 0, 0)  7.6 us
    pallas_call x1, Pallas kernels, backward(): pl.pallas_call(functools.partial(backward_kernel, lay), in_specs=[VMEM] *...  7.35 us
    all_to_all x1, starting transfers between devices, on_device(): got = lax.all_to_all(message, axes, 0, 0)  7.31 us
    pallas_call x1, Pallas kernels, forward(): pl.pallas_call(functools.partial(forward_kernel, lay), in_specs=[SMEM] +...  6.75 us
    pallas_call x1, Pallas kernels, near_field(): pl.pallas_call(functools.partial(near_kernel, len(terms)), in_specs=[VMEM...  5.52 us
    pallas_call x1, Pallas kernels, translate_far(): pl.pallas_call(functools.partial(translate_kernel, lay), in_specs=[VMEM]...  4.6 us
    ppermute x3, starting transfers between devices, answers(): lax.ppermute(half[k], 'ang', [(i, i ^ 2 * k) for i in range(n_ang)])  4.45 us
    all_to_all x1, starting transfers between devices, on_device(): returned = lax.all_to_all(incoming.reshape(lay.n_dev, 8, 128), axes, 0, 0)  3.29 us
  transfers between devices with their start and end apart: 6, of which 3 were waited for; matrix products, arithmetic and copies ran while one was open for 0% of the time, Pallas kernels for 19%

profile of v3, /device:TPU:0, one launch (start us, length us, event | category | flops | bytes accessed | tf_op | source)
XLA Modules:
  0.0 51.9 jit_solution(4519062832608640444)
XLA Ops:
  0.0 0.0 copy-start
  0.0 0.0 copy-start.1
  0.0 6.7 %forward.1 = (s32[32,8,128]{2,1,0:T(8,128)}, f32[8,1536]{1,0:T(8,128)S(1)}, f32[8,1536]{1,0:T(8,128)S(1)}) custom-call(s32[1]{0:T(128)} %bitcast.ang_ref, bf16[2,128,256]{2,1,0:T(8,128)(2,1)} %cur_ref.1, f32[8,1536]{1,0:T(8,128)} %phase_hbm.1, s32[16,128]{1,0:T(8,128)} %bitcast.38, s32[16,128]{1,0:T(8,128)} %bitcast.39, s32[1,40]{1,0:T(1,128)} %bitcast.40, ...), custom_call_target="tpu_custom_call" | custom-call | flops 3000000000 | bytes 9000000 | tf_op jit(solution)/shard_map/forward/pallas_call | solution.py:197
  6.8 0.0 copy-start.2
  6.8 7.3 %all-to-all-start = ((s32[32,8,128]{2,1,0:T(8,128)}), s32[32,8,128]{2,1,0:T(8,128)S(1)}, u32[]{:S(2)}, u32[]{:S(2)}) async-start(s32[32,8,128]{2,1,0:T(8,128)} %get-tuple-element.21), calls=%async_computation | async-start | bytes 262144 | tf_op jit(solution)/shard_map/all_to_all | solution.py:515
  14.1 0.0 copy-done
  14.1 0.1 pad_add_fusion.me_ref
  14.2 7.6 %all-to-all-done.got_ref = s32[32,8,128]{2,1,0:T(8,128)S(1)} async-done(((s32[32,8,128]{2,1,0:T(8,128)}), s32[32,8,128]{2,1,0:T(8,128)S(1)}, u32[]{:S(2)}, u32[]{:S(2)}) %all-to-all-start) | async-done | bytes 131104 | tf_op jit(solution)/shard_map/all_to_all | solution.py:515
  21.8 0.0 copy-done.1
  21.8 0.9 %pick_columns.1 = (bf16[80,256]{1,0:T(8,128)(2,1)S(1)}, bf16[80,256]{1,0:T(8,128)(2,1)S(1)}, bf16[80,256]{1,0:T(8,128)(2,1)S(1)}, bf16[80,256]{1,0:T(8,128)(2,1)...) custom-call(s32[2]{0:T(128)S(1)} %pad_add_fusion.me_ref, ...), custom_call_target="tpu_custom_call" | custom-call | flops 100000000 | bytes 1000000 | tf_op jit(solution)/shard_map/pick_columns/pallas_call | solution.py:411
  22.7 1.3 %collective-permute-start = (bf16[4,80,256]{2,1,0:T(8,128)(2,1)S(1)}, bf16[4,80,256]{2,1,0:T(8,128)(2,1)S(1)}, u32[]{:S(2)}, u32[]{:S(2)}) collective-permute-start(bf16[4,80,256]{2,1,0:T(8,128)(2,1)S(1)} %pad_maximum_fusion), channel_id=1, source_target_pairs={{0,1},{1,0},{2,3},{3,2},{4,5},{5,4},{6,7},{7,6},{8,9},{9,8},{10,11... | collective-permute-start | bytes 491528 | tf_op jit(solution)/shard_map/ppermute | solution.py:425
  24.0 4.6 %translate_far.1 = s32[256,128]{1,0:T(8,128)} custom-call(s32[256,128]{1,0:T(8,128)S(1)} %bitcast.32, f32[96,384]{1,0:T(8,128)S(1)} %bitcast.31), custom_call_target="tpu_custom_call" | custom-call | flops 2000000000 | bytes 1000000 | tf_op jit(solution)/shard_map/translate_far/pallas_call | solution.py:280
  28.6 0.4 collective-permute-done
  29.0 0.6 %collective-permute-start.1 = (bf16[80,256]{1,0:T(8,128)(2,1)S(1)}, bf16[80,256]{1,0:T(8,128)(2,1)S(1)}, u32[]{:S(2)}, u32[]{:S(2)}) collective-permute-start(bf16[80,256]{1,0:T(8,128)(2,1)S(1)} %get-tuple-element.34), channel_id=1, source_target_pairs={{0,2},{1,3},{2,0},{3,1},{4,6},{5,7},{6,4},{7,5},{8,10},{9,11},{10,... | collective-permute-start | bytes 122888 | tf_op jit(solution)/shard_map/ppermute | solution.py:431
  29.7 1.0 %collective-permute-start.2 = (bf16[80,256]{1,0:T(8,128)(2,1)S(1)}, bf16[80,256]{1,0:T(8,128)(2,1)S(1)}, u32[]{:S(2)}, u32[]{:S(2)}) collective-permute-start(bf16[80,256]{1,0:T(8,128)(2,1)S(1)} %get-tuple-element.35), channel_id=1, source_target_pairs={{0,4},{1,5},{2,6},{3,7},{4,0},{5,1},{6,2},{7,3},{8,12},{9,13},{10,... | collective-permute-start | bytes 122888 | tf_op jit(solution)/shard_map/ppermute | solution.py:431
  30.7 2.8 %collective-permute-start.3 = (bf16[80,256]{1,0:T(8,128)(2,1)S(1)}, bf16[80,256]{1,0:T(8,128)(2,1)S(1)}, u32[]{:S(2)}, u32[]{:S(2)}) collective-permute-start(bf16[80,256]{1,0:T(8,128)(2,1)S(1)} %get-tuple-element.36), channel_id=1, source_target_pairs={{0,6},{1,7},{2,4},{3,5},{4,2},{5,3},{6,0},{7,1},{8,14},{9,15},{10,... | collective-permute-start | bytes 122888 | tf_op jit(solution)/shard_map/ppermute | solution.py:431
  33.5 3.3 %all-to-all-start.1 = ((s32[32,8,128]{2,1,0:T(8,128)}), s32[32,8,128]{2,1,0:T(8,128)}, u32[]{:S(2)}, u32[]{:S(2)}) async-start(s32[32,8,128]{2,1,0:T(8,128)} %bitcast.16), calls=%async_computation.1 | async-start | bytes 262144 | tf_op jit(solution)/shard_map/all_to_all | solution.py:526
  36.8 0.0 collective-permute-done.1.refs_2_
  36.8 0.0 collective-permute-done.2.refs_3_
  36.8 0.0 collective-permute-done.3.refs_4_
  36.8 0.0 copy-done.2
  36.8 5.5 %near_field.1.near_ref = f32[2,128,256]{2,1,0:T(8,128)S(1)} custom-call(s32[1,40]{1,0:T(1,128)S(1)} %bitcast.37, bf16[80,256]{1,0:T(8,128)(2,1)S(1)} %get-tuple-element.33.refs_1_, bf16[80,256]{1,0:T(8,128)(2,1)S(1)} %collective-permute-done.1.refs_2_, bf16[80,256]{1,0:T(8,128)(2,1)S(1)} %collective-permute-done.2.refs_3_, ...), custom_call_target="tpu_custom_call" | custom-call | flops 199999995904 | bytes 12000000 | tf_op jit(solution)/shard_map/near_field/pallas_call | solution.py:484
  42.4 2.1 %all-to-all-done.1.got_ref = s32[32,8,128]{2,1,0:T(8,128)} async-done(((s32[32,8,128]{2,1,0:T(8,128)}), s32[32,8,128]{2,1,0:T(8,128)}, u32[]{:S(2)}, u32[]{:S(2)}) %all-to-all-start.1) | async-done | bytes 131104 | tf_op jit(solution)/shard_map/all_to_all | solution.py:526
  44.5 7.4 %backward.1 = f32[2,128,256]{2,1,0:T(8,128)} custom-call(s32[32,8,128]{2,1,0:T(8,128)} %all-to-all-done.1.got_ref, f32[8,1536]{1,0:T(8,128)S(1)} %get-tuple-element.31.cos_ref, f32[8,1536]{1,0:T(8,128)S(1)} %get-tuple-element.32.sin_ref, f32[2,128,256]{2,1,0:T(8,128)S(1)} %near_field.1.near_ref, f32[1536,1024]{1,0:T(8,128)} %interp_hbm.3, ...), custom_call_target="tpu_custom_call" | custom-call | flops 3000000000 | bytes 9000000 | tf_op jit(solution)/shard_map/backward/pallas_call | solution.py:370
  (4 shorter events, 0.1 us)
Async XLA Ops:
  0.0 14.1 %copy-start = (f32[2,316,192]{1,2,0:T(8,128)S(1)}, f32[2,316,192]{1,2,0:T(8,128)}, u32[]{:S(2)}) copy-start(f32[2,316,192]{1,2,0:T(8,128)} %param.19) | copy-start | bytes 1456132
  0.0 21.8 %copy-start.1 = (bf16[2,128,256]{2,1,0:T(8,128)(2,1)S(1)}, bf16[2,128,256]{2,1,0:T(8,128)(2,1)}, u32[]{:S(2)}) copy-start(bf16[2,128,256]{2,1,0:T(8,128)(2,1)} %cur_ref.1) | copy-start | bytes 393220
  6.8 30.1 %copy-start.2 = (s32[40]{0:T(128)S(1)}, s32[40]{0:T(128)}, u32[]{:S(2)}) copy-start(s32[40]{0:T(128)} %param.13) | copy-start | bytes 484
  6.8 15.1 %all-to-all-start = ((s32[32,8,128]{2,1,0:T(8,128)}), s32[32,8,128]{2,1,0:T(8,128)S(1)}, u32[]{:S(2)}, u32[]{:S(2)}) async-start(s32[32,8,128]{2,1,0:T(8,128)} %get-tuple-element.21), calls=%async_computation | async-start | bytes 262144 | tf_op jit(solution)/shard_map/all_to_all | solution.py:515
  22.7 6.3 %collective-permute-start = (bf16[4,80,256]{2,1,0:T(8,128)(2,1)S(1)}, bf16[4,80,256]{2,1,0:T(8,128)(2,1)S(1)}, u32[]{:S(2)}, u32[]{:S(2)}) collective-permute-start(bf16[4,80,256]{2,1,0:T(8,128)(2,1)S(1)} %pad_maximum_fusion), channel_id=1, source_target_pairs={{0,1},{1,0},{2,3},{3,2},{4,5},{5,4},{6,7},{7,6},{8,9},{9,8},{10,11... | collective-permute-start | bytes 491528 | tf_op jit(solution)/shard_map/ppermute | solution.py:425
  29.0 7.8 %collective-permute-start.1 = (bf16[80,256]{1,0:T(8,128)(2,1)S(1)}, bf16[80,256]{1,0:T(8,128)(2,1)S(1)}, u32[]{:S(2)}, u32[]{:S(2)}) collective-permute-start(bf16[80,256]{1,0:T(8,128)(2,1)S(1)} %get-tuple-element.34), channel_id=1, source_target_pairs={{0,2},{1,3},{2,0},{3,1},{4,6},{5,7},{6,4},{7,5},{8,10},{9,11},{10,... | collective-permute-start | bytes 122888 | tf_op jit(solution)/shard_map/ppermute | solution.py:431
  29.7 7.1 %collective-permute-start.2 = (bf16[80,256]{1,0:T(8,128)(2,1)S(1)}, bf16[80,256]{1,0:T(8,128)(2,1)S(1)}, u32[]{:S(2)}, u32[]{:S(2)}) collective-permute-start(bf16[80,256]{1,0:T(8,128)(2,1)S(1)} %get-tuple-element.35), channel_id=1, source_target_pairs={{0,4},{1,5},{2,6},{3,7},{4,0},{5,1},{6,2},{7,3},{8,12},{9,13},{10,... | collective-permute-start | bytes 122888 | tf_op jit(solution)/shard_map/ppermute | solution.py:431
  30.7 6.1 %collective-permute-start.3 = (bf16[80,256]{1,0:T(8,128)(2,1)S(1)}, bf16[80,256]{1,0:T(8,128)(2,1)S(1)}, u32[]{:S(2)}, u32[]{:S(2)}) collective-permute-start(bf16[80,256]{1,0:T(8,128)(2,1)S(1)} %get-tuple-element.36), channel_id=1, source_target_pairs={{0,6},{1,7},{2,4},{3,5},{4,2},{5,3},{6,0},{7,1},{8,14},{9,15},{10,... | collective-permute-start | bytes 122888 | tf_op jit(solution)/shard_map/ppermute | solution.py:431
  33.5 11.0 %all-to-all-start.1 = ((s32[32,8,128]{2,1,0:T(8,128)}), s32[32,8,128]{2,1,0:T(8,128)}, u32[]{:S(2)}, u32[]{:S(2)}) async-start(s32[32,8,128]{2,1,0:T(8,128)} %bitcast.16), calls=%async_computation.1 | async-start | bytes 262144 | tf_op jit(solution)/shard_map/all_to_all | solution.py:526

commit v4 on v3

--- a/solution.py
+++ b/solution.py
@@ -298,8 +298,9 @@
     interp_piece = piece(interp_hbm, interp_ref, interp_sems, 0, ROWS)
     rec_piece = piece(rec_hbm, rec_ref, rec_sems, 1, TILE)
     n_interp, n_rec = interp_sems.shape[0], rec_sems.shape[0]
-    for i in range(3):
-        interp_piece(i).start()
+    order = [(interp_piece, i) for i in range(n_interp)] + [(rec_piece, i) for i in range(n_rec)]
+    for fetch, i in order[:3]:
+        fetch(i).start()
     count = near_ref.shape[1]
     n_par = count // 8
 
@@ -332,15 +333,10 @@
     def leaf_tile(i, carry):
         interp_piece(i).wait()
 
-        @pl.when(i + 3 < n_interp)
-        def _():
-            interp_piece(i + 3).start()
-
-        @pl.when(i + 3 >= n_interp)
-        def _():
-            @pl.when(i + 3 - n_interp < n_rec)
+        for k, (fetch, which) in enumerate(order[3:]):
+            @pl.when(i == min(k, n_interp - 1))
             def _():
-                rec_piece(i + 3 - n_interp).start()
+                fetch(which).start()
 
         at = pl.ds(pl.multiple_of(i * ROWS, ROWS), ROWS)
         in_high, in_low = halves(interp_ref[at, :])
@@ -493,7 +489,7 @@
             pltpu.SemaphoreType.DMA((n_block // here,)),
         ],
         compiler_params=pltpu.CompilerParams(vmem_limit_bytes=VMEM_LIMIT),
-        cost_estimate=pl.CostEstimate(flops=2 * 10**11, bytes_accessed=12 * 10**6, transcendentals=0),
+        cost_estimate=pl.CostEstimate(flops=2 * 10**10, bytes_accessed=12 * 10**6, transcendentals=0),
         name="near_field",
     )(rows, *terms, in_hbm(blocks))
 

time: 52.1 us -> 50.5 us (0.969)
  Pallas kernels: 25.1 us -> 24.2 us
  starting transfers between devices: 16.3 us -> 15.6 us
    pallas_call x1, Pallas kernels: 7.35 us -> 6.48 us  [backward(): pl.pallas_call(functools.partial(backward_kernel, lay), in_specs=[VMEM] *...]
    all_to_all x1, starting transfers between devices: 3.29 us -> 2.58 us  [on_device(): returned = lax.all_to_all(incoming.reshape(lay.n_dev, 8, 128), axes, 0, 0)]
  transfers between devices with their start and end apart: 6 -> 6, of which waited for: 3 -> 4; matrix products, arithmetic and copies ran while one was open for 0% -> 0% of each run, Pallas kernels for 19% -> 20%
where the time goes in v4:
time: 50.5 us; the launch traced here: 50.3 us
  Pallas kernels  24.2 us (48%)
  starting transfers between devices  15.6 us (31%)
  waiting for transfers between devices  10.2 us (20%)
    all_to_all x1, waiting for transfers between devices, on_device(): got = lax.all_to_all(message, axes, 0, 0)  7.6 us
    all_to_all x1, starting transfers between devices, on_device(): got = lax.all_to_all(message, axes, 0, 0)  7.31 us
    pallas_call x1, Pallas kernels, forward(): pl.pallas_call(functools.partial(forward_kernel, lay), in_specs=[SMEM] +...  6.75 us
    pallas_call x1, Pallas kernels, backward(): pl.pallas_call(functools.partial(backward_kernel, lay), in_specs=[VMEM] *...  6.48 us
    pallas_call x1, Pallas kernels, near_field(): pl.pallas_call(functools.partial(near_kernel, len(terms)), in_specs=[VMEM...  5.52 us
    pallas_call x1, Pallas kernels, translate_far(): pl.pallas_call(functools.partial(translate_kernel, lay), in_specs=[VMEM]...  4.6 us
    ppermute x3, starting transfers between devices, answers(): lax.ppermute(half[k], 'ang', [(i, i ^ 2 * k) for i in range(n_ang)])  4.45 us
    all_to_all x1, starting transfers between devices, on_device(): returned = lax.all_to_all(incoming.reshape(lay.n_dev, 8, 128), axes, 0, 0)  2.58 us
  transfers between devices with their start and end apart: 6, of which 4 were waited for; matrix products, arithmetic and copies ran while one was open for 0% of the time, Pallas kernels for 20%

profile of v4, /device:TPU:0, one launch (start us, length us, event | category | flops | bytes accessed | tf_op | source)
XLA Modules:
  0.0 50.3 jit_solution(6581000781844666287)
XLA Ops:
  0.0 0.0 copy-start
  0.0 0.0 copy-start.1
  0.0 6.7 %forward.1 = (s32[32,8,128]{2,1,0:T(8,128)}, f32[8,1536]{1,0:T(8,128)S(1)}, f32[8,1536]{1,0:T(8,128)S(1)}) custom-call(s32[1]{0:T(128)} %bitcast.ang_ref, bf16[2,128,256]{2,1,0:T(8,128)(2,1)} %cur_ref.1, f32[8,1536]{1,0:T(8,128)} %phase_hbm.1, s32[16,128]{1,0:T(8,128)} %bitcast.38, s32[16,128]{1,0:T(8,128)} %bitcast.39, s32[1,40]{1,0:T(1,128)} %bitcast.40, ...), custom_call_target="tpu_custom_call" | custom-call | flops 3000000000 | bytes 9000000 | tf_op jit(solution)/shard_map/forward/pallas_call | solution.py:197
  6.8 0.0 copy-start.2
  6.8 7.3 %all-to-all-start = ((s32[32,8,128]{2,1,0:T(8,128)}), s32[32,8,128]{2,1,0:T(8,128)S(1)}, u32[]{:S(2)}, u32[]{:S(2)}) async-start(s32[32,8,128]{2,1,0:T(8,128)} %get-tuple-element.21), calls=%async_computation | async-start | bytes 262144 | tf_op jit(solution)/shard_map/all_to_all | solution.py:511
  14.1 0.0 copy-done
  14.1 0.1 pad_add_fusion.me_ref
  14.2 7.6 %all-to-all-done.got_ref = s32[32,8,128]{2,1,0:T(8,128)S(1)} async-done(((s32[32,8,128]{2,1,0:T(8,128)}), s32[32,8,128]{2,1,0:T(8,128)S(1)}, u32[]{:S(2)}, u32[]{:S(2)}) %all-to-all-start) | async-done | bytes 131104 | tf_op jit(solution)/shard_map/all_to_all | solution.py:511
  21.8 0.0 copy-done.1
  21.8 0.9 %pick_columns.1 = (bf16[80,256]{1,0:T(8,128)(2,1)S(1)}, bf16[80,256]{1,0:T(8,128)(2,1)S(1)}, bf16[80,256]{1,0:T(8,128)(2,1)S(1)}, bf16[80,256]{1,0:T(8,128)(2,1)...) custom-call(s32[2]{0:T(128)S(1)} %pad_add_fusion.me_ref, ...), custom_call_target="tpu_custom_call" | custom-call | flops 100000000 | bytes 1000000 | tf_op jit(solution)/shard_map/pick_columns/pallas_call | solution.py:407
  22.7 1.3 %collective-permute-start = (bf16[4,80,256]{2,1,0:T(8,128)(2,1)S(1)}, bf16[4,80,256]{2,1,0:T(8,128)(2,1)S(1)}, u32[]{:S(2)}, u32[]{:S(2)}) collective-permute-start(bf16[4,80,256]{2,1,0:T(8,128)(2,1)S(1)} %pad_maximum_fusion), channel_id=1, source_target_pairs={{0,1},{1,0},{2,3},{3,2},{4,5},{5,4},{6,7},{7,6},{8,9},{9,8},{10,11... | collective-permute-start | bytes 491528 | tf_op jit(solution)/shard_map/ppermute | solution.py:421
  24.0 4.6 %translate_far.1 = s32[256,128]{1,0:T(8,128)} custom-call(s32[256,128]{1,0:T(8,128)S(1)} %bitcast.32, f32[96,384]{1,0:T(8,128)S(1)} %bitcast.31), custom_call_target="tpu_custom_call" | custom-call | flops 2000000000 | bytes 1000000 | tf_op jit(solution)/shard_map/translate_far/pallas_call | solution.py:280
  28.6 0.4 collective-permute-done
  29.0 0.6 %collective-permute-start.1 = (bf16[80,256]{1,0:T(8,128)(2,1)S(1)}, bf16[80,256]{1,0:T(8,128)(2,1)S(1)}, u32[]{:S(2)}, u32[]{:S(2)}) collective-permute-start(bf16[80,256]{1,0:T(8,128)(2,1)S(1)} %get-tuple-element.34), channel_id=1, source_target_pairs={{0,2},{1,3},{2,0},{3,1},{4,6},{5,7},{6,4},{7,5},{8,10},{9,11},{10,... | collective-permute-start | bytes 122888 | tf_op jit(solution)/shard_map/ppermute | solution.py:427
  29.7 1.0 %collective-permute-start.2 = (bf16[80,256]{1,0:T(8,128)(2,1)S(1)}, bf16[80,256]{1,0:T(8,128)(2,1)S(1)}, u32[]{:S(2)}, u32[]{:S(2)}) collective-permute-start(bf16[80,256]{1,0:T(8,128)(2,1)S(1)} %get-tuple-element.35), channel_id=1, source_target_pairs={{0,4},{1,5},{2,6},{3,7},{4,0},{5,1},{6,2},{7,3},{8,12},{9,13},{10,... | collective-permute-start | bytes 122888 | tf_op jit(solution)/shard_map/ppermute | solution.py:427
  30.7 2.8 %collective-permute-start.3 = (bf16[80,256]{1,0:T(8,128)(2,1)S(1)}, bf16[80,256]{1,0:T(8,128)(2,1)S(1)}, u32[]{:S(2)}, u32[]{:S(2)}) collective-permute-start(bf16[80,256]{1,0:T(8,128)(2,1)S(1)} %get-tuple-element.36), channel_id=1, source_target_pairs={{0,6},{1,7},{2,4},{3,5},{4,2},{5,3},{6,0},{7,1},{8,14},{9,15},{10,... | collective-permute-start | bytes 122888 | tf_op jit(solution)/shard_map/ppermute | solution.py:427
  33.5 2.6 %all-to-all-start.1 = ((s32[32,8,128]{2,1,0:T(8,128)}), s32[32,8,128]{2,1,0:T(8,128)S(1)}, u32[]{:S(2)}, u32[]{:S(2)}) async-start(s32[32,8,128]{2,1,0:T(8,128)} %bitcast.16), calls=%async_computation.1 | async-start | bytes 262144 | tf_op jit(solution)/shard_map/all_to_all | solution.py:522
  36.1 0.0 collective-permute-done.1.refs_2_
  36.1 0.0 collective-permute-done.2.refs_3_
  36.1 0.4 collective-permute-done.3.refs_4_
  36.5 0.0 copy-done.2
  36.5 5.5 %near_field.1.near_ref = f32[2,128,256]{2,1,0:T(8,128)S(1)} custom-call(s32[1,40]{1,0:T(1,128)S(1)} %bitcast.37, bf16[80,256]{1,0:T(8,128)(2,1)S(1)} %get-tuple-element.33.refs_1_, bf16[80,256]{1,0:T(8,128)(2,1)S(1)} %collective-permute-done.1.refs_2_, bf16[80,256]{1,0:T(8,128)(2,1)S(1)} %collective-permute-done.2.refs_3_, ...), custom_call_target="tpu_custom_call" | custom-call | flops 20000000000 | bytes 12000000 | tf_op jit(solution)/shard_map/near_field/pallas_call | solution.py:480
  42.1 1.8 %all-to-all-done.1.got_ref = s32[32,8,128]{2,1,0:T(8,128)S(1)} async-done(((s32[32,8,128]{2,1,0:T(8,128)}), s32[32,8,128]{2,1,0:T(8,128)S(1)}, u32[]{:S(2)}, u32[]{:S(2)}) %all-to-all-start.1) | async-done | bytes 131104 | tf_op jit(solution)/shard_map/all_to_all | solution.py:522
  43.8 6.5 %backward.1 = f32[2,128,256]{2,1,0:T(8,128)} custom-call(s32[32,8,128]{2,1,0:T(8,128)S(1)} %all-to-all-done.1.got_ref, f32[8,1536]{1,0:T(8,128)S(1)} %get-tuple-element.31.cos_ref, f32[8,1536]{1,0:T(8,128)S(1)} %get-tuple-element.32.sin_ref, f32[2,128,256]{2,1,0:T(8,128)S(1)} %near_field.1.near_ref, f32[1536,1024]{1,0:T(8,128)} %interp_hbm.3, ...), custom_call_target="tpu_custom_call" | custom-call | flops 3000000000 | bytes 9000000 | tf_op jit(solution)/shard_map/backward/pallas_call | solution.py:366
  (4 shorter events, 0.1 us)
Async XLA Ops:
  0.0 14.1 %copy-start = (f32[2,316,192]{1,2,0:T(8,128)S(1)}, f32[2,316,192]{1,2,0:T(8,128)}, u32[]{:S(2)}) copy-start(f32[2,316,192]{1,2,0:T(8,128)} %param.19) | copy-start | bytes 1456132
  0.0 21.8 %copy-start.1 = (bf16[2,128,256]{2,1,0:T(8,128)(2,1)S(1)}, bf16[2,128,256]{2,1,0:T(8,128)(2,1)}, u32[]{:S(2)}) copy-start(bf16[2,128,256]{2,1,0:T(8,128)(2,1)} %cur_ref.1) | copy-start | bytes 393220
  6.8 29.8 %copy-start.2 = (s32[40]{0:T(128)S(1)}, s32[40]{0:T(128)}, u32[]{:S(2)}) copy-start(s32[40]{0:T(128)} %param.13) | copy-start | bytes 484
  6.8 15.1 %all-to-all-start = ((s32[32,8,128]{2,1,0:T(8,128)}), s32[32,8,128]{2,1,0:T(8,128)S(1)}, u32[]{:S(2)}, u32[]{:S(2)}) async-start(s32[32,8,128]{2,1,0:T(8,128)} %get-tuple-element.21), calls=%async_computation | async-start | bytes 262144 | tf_op jit(solution)/shard_map/all_to_all | solution.py:511
  22.7 6.3 %collective-permute-start = (bf16[4,80,256]{2,1,0:T(8,128)(2,1)S(1)}, bf16[4,80,256]{2,1,0:T(8,128)(2,1)S(1)}, u32[]{:S(2)}, u32[]{:S(2)}) collective-permute-start(bf16[4,80,256]{2,1,0:T(8,128)(2,1)S(1)} %pad_maximum_fusion), channel_id=1, source_target_pairs={{0,1},{1,0},{2,3},{3,2},{4,5},{5,4},{6,7},{7,6},{8,9},{9,8},{10,11... | collective-permute-start | bytes 491528 | tf_op jit(solution)/shard_map/ppermute | solution.py:421
  29.0 7.0 %collective-permute-start.1 = (bf16[80,256]{1,0:T(8,128)(2,1)S(1)}, bf16[80,256]{1,0:T(8,128)(2,1)S(1)}, u32[]{:S(2)}, u32[]{:S(2)}) collective-permute-start(bf16[80,256]{1,0:T(8,128)(2,1)S(1)} %get-tuple-element.34), channel_id=1, source_target_pairs={{0,2},{1,3},{2,0},{3,1},{4,6},{5,7},{6,4},{7,5},{8,10},{9,11},{10,... | collective-permute-start | bytes 122888 | tf_op jit(solution)/shard_map/ppermute | solution.py:427
  29.7 6.4 %collective-permute-start.2 = (bf16[80,256]{1,0:T(8,128)(2,1)S(1)}, bf16[80,256]{1,0:T(8,128)(2,1)S(1)}, u32[]{:S(2)}, u32[]{:S(2)}) collective-permute-start(bf16[80,256]{1,0:T(8,128)(2,1)S(1)} %get-tuple-element.35), channel_id=1, source_target_pairs={{0,4},{1,5},{2,6},{3,7},{4,0},{5,1},{6,2},{7,3},{8,12},{9,13},{10,... | collective-permute-start | bytes 122888 | tf_op jit(solution)/shard_map/ppermute | solution.py:427
  30.7 5.8 %collective-permute-start.3 = (bf16[80,256]{1,0:T(8,128)(2,1)S(1)}, bf16[80,256]{1,0:T(8,128)(2,1)S(1)}, u32[]{:S(2)}, u32[]{:S(2)}) collective-permute-start(bf16[80,256]{1,0:T(8,128)(2,1)S(1)} %get-tuple-element.36), channel_id=1, source_target_pairs={{0,6},{1,7},{2,4},{3,5},{4,2},{5,3},{6,0},{7,1},{8,14},{9,15},{10,... | collective-permute-start | bytes 122888 | tf_op jit(solution)/shard_map/ppermute | solution.py:427
  33.5 10.3 %all-to-all-start.1 = ((s32[32,8,128]{2,1,0:T(8,128)}), s32[32,8,128]{2,1,0:T(8,128)S(1)}, u32[]{:S(2)}, u32[]{:S(2)}) async-start(s32[32,8,128]{2,1,0:T(8,128)} %bitcast.16), calls=%async_computation.1 | async-start | bytes 262144 | tf_op jit(solution)/shard_map/all_to_all | solution.py:522

commit v5 on v4

--- a/solution.py
+++ b/solution.py
@@ -416,16 +416,17 @@
 
 
 def swap(picked, n_ang):
-    half = [picked[mask] for mask in range(0, n_ang, 2)]
-    sent = jnp.stack([picked[mask] for mask in range(1, n_ang, 2)])
-    got = lax.ppermute(sent, "ang", [(i, i ^ 1) for i in range(n_ang)])
-    return [one + got[k] for k, one in enumerate(half)]
+    first = 1
+    kept = [mask for mask in range(n_ang) if not mask & first]
+    sent = jnp.stack([picked[mask ^ first] for mask in kept])
+    got = lax.ppermute(sent, "ang", [(i, i ^ first) for i in range(n_ang)])
+    return {mask: picked[mask] + got[k] for k, mask in enumerate(kept)}
 
 
 def answers(half, n_ang):
-    return [half[0]] + [
-        lax.ppermute(half[k], "ang", [(i, i ^ (2 * k)) for i in range(n_ang)]) for k in range(1, len(half))
-    ]
+    masks = sorted(half)
+    order = [masks[k ^ (k >> 1)] for k in range(1, len(masks))]
+    return [half[0]] + [lax.ppermute(half[mask], "ang", [(i, i ^ mask) for i in range(n_ang)]) for mask in order]
 
 
 def near_kernel(n_term, *refs):

time: 50.5 us -> 49.7 us (0.984)
  starting transfers between devices: 15.6 us -> 14.8 us
    ppermute x4, waiting for transfers between devices: 0.83 us -> 1.98 us  [the longest x3 1.59 us: answers(): lax.ppermute(half[mask], 'ang', [(i, i ^ mask) for i in range(n_ang)])]
    all_to_all x1, waiting for transfers between devices: 1.75 us -> 0.6 us  [on_device(): returned = lax.all_to_all(incoming.reshape(lay.n_dev, 8, 128), axes, 0, 0)]
    ppermute x4, starting transfers between devices: 5.74 us -> 4.84 us  [the longest x3 3.55 us: answers(): lax.ppermute(half[mask], 'ang', [(i, i ^ mask) for i in range(n_ang)])]
  transfers between devices with their start and end apart: 6 -> 6, of which waited for: 4 -> 5; matrix products, arithmetic and copies ran while one was open for 0% -> 0% of each run, Pallas kernels for 20% -> 20%
where the time goes in v5:
time: 49.7 us; the launch traced here: 49.5 us
  Pallas kernels  24.2 us (49%)
  starting transfers between devices  14.8 us (30%)
  waiting for transfers between devices  10.2 us (21%)
    all_to_all x1, waiting for transfers between devices, on_device(): got = lax.all_to_all(message, axes, 0, 0)  7.6 us
    all_to_all x1, starting transfers between devices, on_device(): got = lax.all_to_all(message, axes, 0, 0)  7.31 us
    pallas_call x1, Pallas kernels, forward(): pl.pallas_call(functools.partial(forward_kernel, lay), in_specs=[SMEM] +...  6.75 us
    pallas_call x1, Pallas kernels, backward(): pl.pallas_call(functools.partial(backward_kernel, lay), in_specs=[VMEM] *...  6.48 us
    pallas_call x1, Pallas kernels, near_field(): pl.pallas_call(functools.partial(near_kernel, len(terms)), in_specs=[VMEM...  5.52 us
    pallas_call x1, Pallas kernels, translate_far(): pl.pallas_call(functools.partial(translate_kernel, lay), in_specs=[VMEM]...  4.6 us
    ppermute x3, starting transfers between devices, answers(): lax.ppermute(half[mask], 'ang', [(i, i ^ mask) for i in range(n_ang)])  3.55 us
    all_to_all x1, starting transfers between devices, on_device(): returned = lax.all_to_all(incoming.reshape(lay.n_dev, 8, 128), axes, 0, 0)  2.63 us
  transfers between devices with their start and end apart: 6, of which 5 were waited for; matrix products, arithmetic and copies ran while one was open for 0% of the time, Pallas kernels for 20%

profile of v5, /device:TPU:0, one launch (start us, length us, event | category | flops | bytes accessed | tf_op | source)
XLA Modules:
  0.0 49.5 jit_solution(9479725061027254574)
XLA Ops:
  0.0 0.0 copy-start
  0.0 0.0 copy-start.1
  0.0 6.7 %forward.1 = (s32[32,8,128]{2,1,0:T(8,128)}, f32[8,1536]{1,0:T(8,128)S(1)}, f32[8,1536]{1,0:T(8,128)S(1)}) custom-call(s32[1]{0:T(128)} %bitcast.ang_ref, bf16[2,128,256]{2,1,0:T(8,128)(2,1)} %cur_ref.1, f32[8,1536]{1,0:T(8,128)} %phase_hbm.1, s32[16,128]{1,0:T(8,128)} %bitcast.38, s32[16,128]{1,0:T(8,128)} %bitcast.39, s32[1,40]{1,0:T(1,128)} %bitcast.40, ...), custom_call_target="tpu_custom_call" | custom-call | flops 3000000000 | bytes 9000000 | tf_op jit(solution)/shard_map/forward/pallas_call | solution.py:197
  6.8 0.0 copy-start.2
  6.8 7.3 %all-to-all-start = ((s32[32,8,128]{2,1,0:T(8,128)}), s32[32,8,128]{2,1,0:T(8,128)S(1)}, u32[]{:S(2)}, u32[]{:S(2)}) async-start(s32[32,8,128]{2,1,0:T(8,128)} %get-tuple-element.21), calls=%async_computation | async-start | bytes 262144 | tf_op jit(solution)/shard_map/all_to_all | solution.py:512
  14.1 0.0 copy-done
  14.1 0.1 pad_add_fusion.me_ref
  14.2 7.6 %all-to-all-done.got_ref = s32[32,8,128]{2,1,0:T(8,128)S(1)} async-done(((s32[32,8,128]{2,1,0:T(8,128)}), s32[32,8,128]{2,1,0:T(8,128)S(1)}, u32[]{:S(2)}, u32[]{:S(2)}) %all-to-all-start) | async-done | bytes 131104 | tf_op jit(solution)/shard_map/all_to_all | solution.py:512
  21.8 0.0 copy-done.1
  21.8 0.9 %pick_columns.1 = (bf16[80,256]{1,0:T(8,128)(2,1)S(1)}, bf16[80,256]{1,0:T(8,128)(2,1)S(1)}, bf16[80,256]{1,0:T(8,128)(2,1)S(1)}, bf16[80,256]{1,0:T(8,128)(2,1)...) custom-call(s32[2]{0:T(128)S(1)} %pad_add_fusion.me_ref, ...), custom_call_target="tpu_custom_call" | custom-call | flops 100000000 | bytes 1000000 | tf_op jit(solution)/shard_map/pick_columns/pallas_call | solution.py:407
  22.7 1.3 %collective-permute-start = (bf16[4,80,256]{2,1,0:T(8,128)(2,1)S(1)}, bf16[4,80,256]{2,1,0:T(8,128)(2,1)S(1)}, u32[]{:S(2)}, u32[]{:S(2)}) collective-permute-start(bf16[4,80,256]{2,1,0:T(8,128)(2,1)S(1)} %pad_maximum_fusion), channel_id=1, source_target_pairs={{0,1},{1,0},{2,3},{3,2},{4,5},{5,4},{6,7},{7,6},{8,9},{9,8},{10,11... | collective-permute-start | bytes 491528 | tf_op jit(solution)/shard_map/ppermute | solution.py:422
  24.0 4.6 %translate_far.1 = s32[256,128]{1,0:T(8,128)} custom-call(s32[256,128]{1,0:T(8,128)S(1)} %bitcast.32, f32[96,384]{1,0:T(8,128)S(1)} %bitcast.31), custom_call_target="tpu_custom_call" | custom-call | flops 2000000000 | bytes 1000000 | tf_op jit(solution)/shard_map/translate_far/pallas_call | solution.py:280
  28.6 0.4 collective-permute-done
  29.0 0.6 %collective-permute-start.1 = (bf16[80,256]{1,0:T(8,128)(2,1)S(1)}, bf16[80,256]{1,0:T(8,128)(2,1)S(1)}, u32[]{:S(2)}, u32[]{:S(2)}) collective-permute-start(bf16[80,256]{1,0:T(8,128)(2,1)S(1)} %get-tuple-element.34), channel_id=1, source_target_pairs={{0,2},{1,3},{2,0},{3,1},{4,6},{5,7},{6,4},{7,5},{8,10},{9,11},{10,... | collective-permute-start | bytes 122888 | tf_op jit(solution)/shard_map/ppermute | solution.py:429
  29.7 2.2 %collective-permute-start.2 = (bf16[80,256]{1,0:T(8,128)(2,1)S(1)}, bf16[80,256]{1,0:T(8,128)(2,1)S(1)}, u32[]{:S(2)}, u32[]{:S(2)}) collective-permute-start(bf16[80,256]{1,0:T(8,128)(2,1)S(1)} %get-tuple-element.35), channel_id=1, source_target_pairs={{0,6},{1,7},{2,4},{3,5},{4,2},{5,3},{6,0},{7,1},{8,14},{9,15},{10,... | collective-permute-start | bytes 122888 | tf_op jit(solution)/shard_map/ppermute | solution.py:429
  31.9 0.7 %collective-permute-start.3 = (bf16[80,256]{1,0:T(8,128)(2,1)S(1)}, bf16[80,256]{1,0:T(8,128)(2,1)S(1)}, u32[]{:S(2)}, u32[]{:S(2)}) collective-permute-start(bf16[80,256]{1,0:T(8,128)(2,1)S(1)} %get-tuple-element.36), channel_id=1, source_target_pairs={{0,4},{1,5},{2,6},{3,7},{4,0},{5,1},{6,2},{7,3},{8,12},{9,13},{10,... | collective-permute-start | bytes 122888 | tf_op jit(solution)/shard_map/ppermute | solution.py:429
  32.6 2.6 %all-to-all-start.1 = ((s32[32,8,128]{2,1,0:T(8,128)}), s32[32,8,128]{2,1,0:T(8,128)S(1)}, u32[]{:S(2)}, u32[]{:S(2)}) async-start(s32[32,8,128]{2,1,0:T(8,128)} %bitcast.16), calls=%async_computation.1 | async-start | bytes 262144 | tf_op jit(solution)/shard_map/all_to_all | solution.py:523
  35.2 0.0 collective-permute-done.1.refs_2_
  35.2 0.2 collective-permute-done.2.refs_3_
  35.5 1.3 %collective-permute-done.3.refs_4_ = bf16[80,256]{1,0:T(8,128)(2,1)S(1)} collective-permute-done((bf16[80,256]{1,0:T(8,128)(2,1)S(1)}, bf16[80,256]{1,0:T(8,128)(2,1)S(1)}, u32[]{:S(2)}, u32[]{:S(2)}) %collective-permute-start.3) | collective-permute-done | bytes 40992 | tf_op jit(solution)/shard_map/ppermute | solution.py:429
  36.8 0.0 copy-done.2
  36.8 5.5 %near_field.1.near_ref = f32[2,128,256]{2,1,0:T(8,128)S(1)} custom-call(s32[1,40]{1,0:T(1,128)S(1)} %bitcast.37, bf16[80,256]{1,0:T(8,128)(2,1)S(1)} %get-tuple-element.33.refs_1_, bf16[80,256]{1,0:T(8,128)(2,1)S(1)} %collective-permute-done.1.refs_2_, bf16[80,256]{1,0:T(8,128)(2,1)S(1)} %collective-permute-done.2.refs_3_, ...), custom_call_target="tpu_custom_call" | custom-call | flops 20000000000 | bytes 12000000 | tf_op jit(solution)/shard_map/near_field/pallas_call | solution.py:481
  42.4 0.6 %all-to-all-done.1.got_ref = s32[32,8,128]{2,1,0:T(8,128)S(1)} async-done(((s32[32,8,128]{2,1,0:T(8,128)}), s32[32,8,128]{2,1,0:T(8,128)S(1)}, u32[]{:S(2)}, u32[]{:S(2)}) %all-to-all-start.1) | async-done | bytes 131104 | tf_op jit(solution)/shard_map/all_to_all | solution.py:523
  43.0 6.5 %backward.1 = f32[2,128,256]{2,1,0:T(8,128)} custom-call(s32[32,8,128]{2,1,0:T(8,128)S(1)} %all-to-all-done.1.got_ref, f32[8,1536]{1,0:T(8,128)S(1)} %get-tuple-element.31.cos_ref, f32[8,1536]{1,0:T(8,128)S(1)} %get-tuple-element.32.sin_ref, f32[2,128,256]{2,1,0:T(8,128)S(1)} %near_field.1.near_ref, f32[1536,1024]{1,0:T(8,128)} %interp_hbm.3, ...), custom_call_target="tpu_custom_call" | custom-call | flops 3000000000 | bytes 9000000 | tf_op jit(solution)/shard_map/backward/pallas_call | solution.py:366
  (4 shorter events, 0.1 us)
Async XLA Ops:
  0.0 14.1 %copy-start = (f32[2,316,192]{1,2,0:T(8,128)S(1)}, f32[2,316,192]{1,2,0:T(8,128)}, u32[]{:S(2)}) copy-start(f32[2,316,192]{1,2,0:T(8,128)} %param.19) | copy-start | bytes 1456132
  0.0 21.8 %copy-start.1 = (bf16[2,128,256]{2,1,0:T(8,128)(2,1)S(1)}, bf16[2,128,256]{2,1,0:T(8,128)(2,1)}, u32[]{:S(2)}) copy-start(bf16[2,128,256]{2,1,0:T(8,128)(2,1)} %cur_ref.1) | copy-start | bytes 393220
  6.8 30.1 %copy-start.2 = (s32[40]{0:T(128)S(1)}, s32[40]{0:T(128)}, u32[]{:S(2)}) copy-start(s32[40]{0:T(128)} %param.13) | copy-start | bytes 484
  6.8 15.1 %all-to-all-start = ((s32[32,8,128]{2,1,0:T(8,128)}), s32[32,8,128]{2,1,0:T(8,128)S(1)}, u32[]{:S(2)}, u32[]{:S(2)}) async-start(s32[32,8,128]{2,1,0:T(8,128)} %get-tuple-element.21), calls=%async_computation | async-start | bytes 262144 | tf_op jit(solution)/shard_map/all_to_all | solution.py:512
  22.7 6.3 %collective-permute-start = (bf16[4,80,256]{2,1,0:T(8,128)(2,1)S(1)}, bf16[4,80,256]{2,1,0:T(8,128)(2,1)S(1)}, u32[]{:S(2)}, u32[]{:S(2)}) collective-permute-start(bf16[4,80,256]{2,1,0:T(8,128)(2,1)S(1)} %pad_maximum_fusion), channel_id=1, source_target_pairs={{0,1},{1,0},{2,3},{3,2},{4,5},{5,4},{6,7},{7,6},{8,9},{9,8},{10,11... | collective-permute-start | bytes 491528 | tf_op jit(solution)/shard_map/ppermute | solution.py:422
  29.0 6.2 %collective-permute-start.1 = (bf16[80,256]{1,0:T(8,128)(2,1)S(1)}, bf16[80,256]{1,0:T(8,128)(2,1)S(1)}, u32[]{:S(2)}, u32[]{:S(2)}) collective-permute-start(bf16[80,256]{1,0:T(8,128)(2,1)S(1)} %get-tuple-element.34), channel_id=1, source_target_pairs={{0,2},{1,3},{2,0},{3,1},{4,6},{5,7},{6,4},{7,5},{8,10},{9,11},{10,... | collective-permute-start | bytes 122888 | tf_op jit(solution)/shard_map/ppermute | solution.py:429
  29.7 5.8 %collective-permute-start.2 = (bf16[80,256]{1,0:T(8,128)(2,1)S(1)}, bf16[80,256]{1,0:T(8,128)(2,1)S(1)}, u32[]{:S(2)}, u32[]{:S(2)}) collective-permute-start(bf16[80,256]{1,0:T(8,128)(2,1)S(1)} %get-tuple-element.35), channel_id=1, source_target_pairs={{0,6},{1,7},{2,4},{3,5},{4,2},{5,3},{6,0},{7,1},{8,14},{9,15},{10,... | collective-permute-start | bytes 122888 | tf_op jit(solution)/shard_map/ppermute | solution.py:429
  31.9 4.9 %collective-permute-start.3 = (bf16[80,256]{1,0:T(8,128)(2,1)S(1)}, bf16[80,256]{1,0:T(8,128)(2,1)S(1)}, u32[]{:S(2)}, u32[]{:S(2)}) collective-permute-start(bf16[80,256]{1,0:T(8,128)(2,1)S(1)} %get-tuple-element.36), channel_id=1, source_target_pairs={{0,4},{1,5},{2,6},{3,7},{4,0},{5,1},{6,2},{7,3},{8,12},{9,13},{10,... | collective-permute-start | bytes 122888 | tf_op jit(solution)/shard_map/ppermute | solution.py:429
  32.6 10.4 %all-to-all-start.1 = ((s32[32,8,128]{2,1,0:T(8,128)}), s32[32,8,128]{2,1,0:T(8,128)S(1)}, u32[]{:S(2)}, u32[]{:S(2)}) async-start(s32[32,8,128]{2,1,0:T(8,128)} %bitcast.16), calls=%async_computation.1 | async-start | bytes 262144 | tf_op jit(solution)/shard_map/all_to_all | solution.py:523

commit v6 on v5

--- a/solution.py
+++ b/solution.py
@@ -57,7 +57,7 @@
 
 
 def exponent(largest):
-    return jnp.ceil(8.0 * jnp.log2(jnp.maximum(largest, 1e-30)))
+    return jnp.ceil(8.0 * jnp.log2(jnp.maximum(largest, 1e-37)))
 
 
 def scale_of(eighths):
@@ -66,14 +66,13 @@
 
 def pack(re, im, scale):
     def grid(x):
-        return jnp.clip(jnp.round(x * (32767.0 / scale)), -32767.0, 32767.0).astype(jnp.int32)
+        return jnp.clip(jnp.round(x * (1.0 / scale) * 32767.0), -32767.0, 32767.0).astype(jnp.int32)
     return jnp.bitwise_or(jnp.left_shift(grid(re), 16), jnp.bitwise_and(grid(im), 65535))
 
 
 def unpack(words, scale):
-    step = scale * (1.0 / 32767.0)
-    re = jnp.right_shift(words, 16).astype(F32) * step
-    im = jnp.right_shift(jnp.left_shift(words, 16), 16).astype(F32) * step
+    re = jnp.right_shift(words, 16).astype(F32) * (1.0 / 32767.0) * scale
+    im = jnp.right_shift(jnp.left_shift(words, 16), 16).astype(F32) * (1.0 / 32767.0) * scale
     return re, im
 
 

time: 49.7 us -> 49.8 us (level)
  no operation moved by 1% of the time
where the time goes in v6:
time: 49.8 us; the launch traced here: 49.5 us
  Pallas kernels  24.3 us (49%)
  starting transfers between devices  14.8 us (30%)
  waiting for transfers between devices  10.2 us (20%)
    all_to_all x1, waiting for transfers between devices, on_device(): got = lax.all_to_all(message, axes, 0, 0)  7.6 us
    all_to_all x1, starting transfers between devices, on_device(): got = lax.all_to_all(message, axes, 0, 0)  7.31 us
    pallas_call x1, Pallas kernels, forward(): pl.pallas_call(functools.partial(forward_kernel, lay), in_specs=[SMEM] +...  6.75 us
    pallas_call x1, Pallas kernels, backward(): pl.pallas_call(functools.partial(backward_kernel, lay), in_specs=[VMEM] *...  6.55 us
    pallas_call x1, Pallas kernels, near_field(): pl.pallas_call(functools.partial(near_kernel, len(terms)), in_specs=[VMEM...  5.52 us
    pallas_call x1, Pallas kernels, translate_far(): pl.pallas_call(functools.partial(translate_kernel, lay), in_specs=[VMEM]...  4.61 us
    ppermute x3, starting transfers between devices, answers(): lax.ppermute(half[mask], 'ang', [(i, i ^ mask) for i in range(n_ang)])  3.55 us
    all_to_all x1, starting transfers between devices, on_device(): returned = lax.all_to_all(incoming.reshape(lay.n_dev, 8, 128), axes, 0, 0)  2.63 us
  transfers between devices with their start and end apart: 6, of which 5 were waited for; matrix products, arithmetic and copies ran while one was open for 0% of the time, Pallas kernels for 20%

profile of v6, /device:TPU:0, one launch (start us, length us, event | category | flops | bytes accessed | tf_op | source)
XLA Modules:
  0.0 49.5 jit_solution(6974080017930641276)
XLA Ops:
  0.0 0.0 copy-start
  0.0 0.0 copy-start.1
  0.0 6.7 %forward.1 = (s32[32,8,128]{2,1,0:T(8,128)}, f32[8,1536]{1,0:T(8,128)S(1)}, f32[8,1536]{1,0:T(8,128)S(1)}) custom-call(s32[1]{0:T(128)} %bitcast.ang_ref, bf16[2,128,256]{2,1,0:T(8,128)(2,1)} %cur_ref.1, f32[8,1536]{1,0:T(8,128)} %phase_hbm.1, s32[16,128]{1,0:T(8,128)} %bitcast.38, s32[16,128]{1,0:T(8,128)} %bitcast.39, s32[1,40]{1,0:T(1,128)} %bitcast.40, ...), custom_call_target="tpu_custom_call" | custom-call | flops 3000000000 | bytes 9000000 | tf_op jit(solution)/shard_map/forward/pallas_call | solution.py:196
  6.8 0.0 copy-start.2
  6.8 7.3 %all-to-all-start = ((s32[32,8,128]{2,1,0:T(8,128)}), s32[32,8,128]{2,1,0:T(8,128)S(1)}, u32[]{:S(2)}, u32[]{:S(2)}) async-start(s32[32,8,128]{2,1,0:T(8,128)} %get-tuple-element.21), calls=%async_computation | async-start | bytes 262144 | tf_op jit(solution)/shard_map/all_to_all | solution.py:511
  14.1 0.0 copy-done
  14.1 0.1 pad_add_fusion.me_ref
  14.2 7.6 %all-to-all-done.got_ref = s32[32,8,128]{2,1,0:T(8,128)S(1)} async-done(((s32[32,8,128]{2,1,0:T(8,128)}), s32[32,8,128]{2,1,0:T(8,128)S(1)}, u32[]{:S(2)}, u32[]{:S(2)}) %all-to-all-start) | async-done | bytes 131104 | tf_op jit(solution)/shard_map/all_to_all | solution.py:511
  21.8 0.0 copy-done.1
  21.8 0.9 %pick_columns.1 = (bf16[80,256]{1,0:T(8,128)(2,1)S(1)}, bf16[80,256]{1,0:T(8,128)(2,1)S(1)}, bf16[80,256]{1,0:T(8,128)(2,1)S(1)}, bf16[80,256]{1,0:T(8,128)(2,1)...) custom-call(s32[2]{0:T(128)S(1)} %pad_add_fusion.me_ref, ...), custom_call_target="tpu_custom_call" | custom-call | flops 100000000 | bytes 1000000 | tf_op jit(solution)/shard_map/pick_columns/pallas_call | solution.py:406
  22.7 1.3 %collective-permute-start = (bf16[4,80,256]{2,1,0:T(8,128)(2,1)S(1)}, bf16[4,80,256]{2,1,0:T(8,128)(2,1)S(1)}, u32[]{:S(2)}, u32[]{:S(2)}) collective-permute-start(bf16[4,80,256]{2,1,0:T(8,128)(2,1)S(1)} %pad_maximum_fusion), channel_id=1, source_target_pairs={{0,1},{1,0},{2,3},{3,2},{4,5},{5,4},{6,7},{7,6},{8,9},{9,8},{10,11... | collective-permute-start | bytes 491528 | tf_op jit(solution)/shard_map/ppermute | solution.py:421
  24.0 4.6 %translate_far.1 = s32[256,128]{1,0:T(8,128)} custom-call(s32[256,128]{1,0:T(8,128)S(1)} %bitcast.32, f32[96,384]{1,0:T(8,128)S(1)} %bitcast.31), custom_call_target="tpu_custom_call" | custom-call | flops 2000000000 | bytes 1000000 | tf_op jit(solution)/shard_map/translate_far/pallas_call | solution.py:279
  28.6 0.4 collective-permute-done
  29.0 0.6 %collective-permute-start.1 = (bf16[80,256]{1,0:T(8,128)(2,1)S(1)}, bf16[80,256]{1,0:T(8,128)(2,1)S(1)}, u32[]{:S(2)}, u32[]{:S(2)}) collective-permute-start(bf16[80,256]{1,0:T(8,128)(2,1)S(1)} %get-tuple-element.34), channel_id=1, source_target_pairs={{0,2},{1,3},{2,0},{3,1},{4,6},{5,7},{6,4},{7,5},{8,10},{9,11},{10,... | collective-permute-start | bytes 122888 | tf_op jit(solution)/shard_map/ppermute | solution.py:428
  29.7 2.2 %collective-permute-start.2 = (bf16[80,256]{1,0:T(8,128)(2,1)S(1)}, bf16[80,256]{1,0:T(8,128)(2,1)S(1)}, u32[]{:S(2)}, u32[]{:S(2)}) collective-permute-start(bf16[80,256]{1,0:T(8,128)(2,1)S(1)} %get-tuple-element.35), channel_id=1, source_target_pairs={{0,6},{1,7},{2,4},{3,5},{4,2},{5,3},{6,0},{7,1},{8,14},{9,15},{10,... | collective-permute-start | bytes 122888 | tf_op jit(solution)/shard_map/ppermute | solution.py:428
  31.9 0.7 %collective-permute-start.3 = (bf16[80,256]{1,0:T(8,128)(2,1)S(1)}, bf16[80,256]{1,0:T(8,128)(2,1)S(1)}, u32[]{:S(2)}, u32[]{:S(2)}) collective-permute-start(bf16[80,256]{1,0:T(8,128)(2,1)S(1)} %get-tuple-element.36), channel_id=1, source_target_pairs={{0,4},{1,5},{2,6},{3,7},{4,0},{5,1},{6,2},{7,3},{8,12},{9,13},{10,... | collective-permute-start | bytes 122888 | tf_op jit(solution)/shard_map/ppermute | solution.py:428
  32.6 2.6 %all-to-all-start.1 = ((s32[32,8,128]{2,1,0:T(8,128)}), s32[32,8,128]{2,1,0:T(8,128)S(1)}, u32[]{:S(2)}, u32[]{:S(2)}) async-start(s32[32,8,128]{2,1,0:T(8,128)} %bitcast.16), calls=%async_computation.1 | async-start | bytes 262144 | tf_op jit(solution)/shard_map/all_to_all | solution.py:522
  35.2 0.0 collective-permute-done.1.refs_2_
  35.2 0.2 collective-permute-done.2.refs_3_
  35.5 1.3 %collective-permute-done.3.refs_4_ = bf16[80,256]{1,0:T(8,128)(2,1)S(1)} collective-permute-done((bf16[80,256]{1,0:T(8,128)(2,1)S(1)}, bf16[80,256]{1,0:T(8,128)(2,1)S(1)}, u32[]{:S(2)}, u32[]{:S(2)}) %collective-permute-start.3) | collective-permute-done | bytes 40992 | tf_op jit(solution)/shard_map/ppermute | solution.py:428
  36.8 0.0 copy-done.2
  36.8 5.5 %near_field.1.near_ref = f32[2,128,256]{2,1,0:T(8,128)S(1)} custom-call(s32[1,40]{1,0:T(1,128)S(1)} %bitcast.37, bf16[80,256]{1,0:T(8,128)(2,1)S(1)} %get-tuple-element.33.refs_1_, bf16[80,256]{1,0:T(8,128)(2,1)S(1)} %collective-permute-done.1.refs_2_, bf16[80,256]{1,0:T(8,128)(2,1)S(1)} %collective-permute-done.2.refs_3_, ...), custom_call_target="tpu_custom_call" | custom-call | flops 20000000000 | bytes 12000000 | tf_op jit(solution)/shard_map/near_field/pallas_call | solution.py:480
  42.4 0.6 %all-to-all-done.1.got_ref = s32[32,8,128]{2,1,0:T(8,128)S(1)} async-done(((s32[32,8,128]{2,1,0:T(8,128)}), s32[32,8,128]{2,1,0:T(8,128)S(1)}, u32[]{:S(2)}, u32[]{:S(2)}) %all-to-all-start.1) | async-done | bytes 131104 | tf_op jit(solution)/shard_map/all_to_all | solution.py:522
  43.0 6.6 %backward.1 = f32[2,128,256]{2,1,0:T(8,128)} custom-call(s32[32,8,128]{2,1,0:T(8,128)S(1)} %all-to-all-done.1.got_ref, f32[8,1536]{1,0:T(8,128)S(1)} %get-tuple-element.31.cos_ref, f32[8,1536]{1,0:T(8,128)S(1)} %get-tuple-element.32.sin_ref, f32[2,128,256]{2,1,0:T(8,128)S(1)} %near_field.1.near_ref, f32[1536,1024]{1,0:T(8,128)} %interp_hbm.3, ...), custom_call_target="tpu_custom_call" | custom-call | flops 3000000000 | bytes 9000000 | tf_op jit(solution)/shard_map/backward/pallas_call | solution.py:365
  (4 shorter events, 0.1 us)
Async XLA Ops:
  0.0 14.1 %copy-start = (f32[2,316,192]{1,2,0:T(8,128)S(1)}, f32[2,316,192]{1,2,0:T(8,128)}, u32[]{:S(2)}) copy-start(f32[2,316,192]{1,2,0:T(8,128)} %param.19) | copy-start | bytes 1456132
  0.0 21.8 %copy-start.1 = (bf16[2,128,256]{2,1,0:T(8,128)(2,1)S(1)}, bf16[2,128,256]{2,1,0:T(8,128)(2,1)}, u32[]{:S(2)}) copy-start(bf16[2,128,256]{2,1,0:T(8,128)(2,1)} %cur_ref.1) | copy-start | bytes 393220
  6.8 30.1 %copy-start.2 = (s32[40]{0:T(128)S(1)}, s32[40]{0:T(128)}, u32[]{:S(2)}) copy-start(s32[40]{0:T(128)} %param.13) | copy-start | bytes 484
  6.8 15.1 %all-to-all-start = ((s32[32,8,128]{2,1,0:T(8,128)}), s32[32,8,128]{2,1,0:T(8,128)S(1)}, u32[]{:S(2)}, u32[]{:S(2)}) async-start(s32[32,8,128]{2,1,0:T(8,128)} %get-tuple-element.21), calls=%async_computation | async-start | bytes 262144 | tf_op jit(solution)/shard_map/all_to_all | solution.py:511
  22.7 6.3 %collective-permute-start = (bf16[4,80,256]{2,1,0:T(8,128)(2,1)S(1)}, bf16[4,80,256]{2,1,0:T(8,128)(2,1)S(1)}, u32[]{:S(2)}, u32[]{:S(2)}) collective-permute-start(bf16[4,80,256]{2,1,0:T(8,128)(2,1)S(1)} %pad_maximum_fusion), channel_id=1, source_target_pairs={{0,1},{1,0},{2,3},{3,2},{4,5},{5,4},{6,7},{7,6},{8,9},{9,8},{10,11... | collective-permute-start | bytes 491528 | tf_op jit(solution)/shard_map/ppermute | solution.py:421
  29.0 6.2 %collective-permute-start.1 = (bf16[80,256]{1,0:T(8,128)(2,1)S(1)}, bf16[80,256]{1,0:T(8,128)(2,1)S(1)}, u32[]{:S(2)}, u32[]{:S(2)}) collective-permute-start(bf16[80,256]{1,0:T(8,128)(2,1)S(1)} %get-tuple-element.34), channel_id=1, source_target_pairs={{0,2},{1,3},{2,0},{3,1},{4,6},{5,7},{6,4},{7,5},{8,10},{9,11},{10,... | collective-permute-start | bytes 122888 | tf_op jit(solution)/shard_map/ppermute | solution.py:428
  29.7 5.8 %collective-permute-start.2 = (bf16[80,256]{1,0:T(8,128)(2,1)S(1)}, bf16[80,256]{1,0:T(8,128)(2,1)S(1)}, u32[]{:S(2)}, u32[]{:S(2)}) collective-permute-start(bf16[80,256]{1,0:T(8,128)(2,1)S(1)} %get-tuple-element.35), channel_id=1, source_target_pairs={{0,6},{1,7},{2,4},{3,5},{4,2},{5,3},{6,0},{7,1},{8,14},{9,15},{10,... | collective-permute-start | bytes 122888 | tf_op jit(solution)/shard_map/ppermute | solution.py:428
  31.9 4.9 %collective-permute-start.3 = (bf16[80,256]{1,0:T(8,128)(2,1)S(1)}, bf16[80,256]{1,0:T(8,128)(2,1)S(1)}, u32[]{:S(2)}, u32[]{:S(2)}) collective-permute-start(bf16[80,256]{1,0:T(8,128)(2,1)S(1)} %get-tuple-element.36), channel_id=1, source_target_pairs={{0,4},{1,5},{2,6},{3,7},{4,0},{5,1},{6,2},{7,3},{8,12},{9,13},{10,... | collective-permute-start | bytes 122888 | tf_op jit(solution)/shard_map/ppermute | solution.py:428
  32.6 10.4 %all-to-all-start.1 = ((s32[32,8,128]{2,1,0:T(8,128)}), s32[32,8,128]{2,1,0:T(8,128)S(1)}, u32[]{:S(2)}, u32[]{:S(2)}) async-start(s32[32,8,128]{2,1,0:T(8,128)} %bitcast.16), calls=%async_computation.1 | async-start | bytes 262144 | tf_op jit(solution)/shard_map/all_to_all | solution.py:522
